TPU v7x, 128 devices: a whole 4x4x4 slice. The times are simulated.
128 devices in a mesh: role: 2 (over core), dev: 64 (over z, y, x).
Axes of the slice: x: 4, y: 4, z: 4, core: 2. Of those that a mesh axis runs over, the one named last changes fastest.
Arguments:
- hidden_in: bfloat16 [512, 7168], P('dev'), may hold values from -250 to 250
- expert_ids: int32 [512, 8], P('dev'), may hold values from 0 to 15, all different within a row
- gate_values: float32 [512, 8], P('dev'), may hold values from 0.2 to 2
- ffn_gain: float32 [7168], replicated, may hold values from 0.25 to 1.75
- w_gate: bfloat16 [7168, 32768], P(None, 'dev'), may hold values from -0.0625 to 0.0625
- w_up: bfloat16 [7168, 32768], P(None, 'dev'), may hold values from -0.0625 to 0.0625
- w_down: bfloat16 [32768, 7168], P('dev'), may hold values from -0.125 to 0.125
- attn_gain: float32 [7168], replicated, may hold values from 0.25 to 1.75
- w_latent: bfloat16 [7168, 576], P('dev'), may hold values from -2 to 2
- kv_gain: float32 [512], replicated, may hold values from 0.25 to 1.75
- queries: bfloat16 [512, 128, 576], P('dev'), may hold values from -13 to 13
- cache: bfloat16 [512, 256, 576], P('dev'), may hold values from -6 to 6
- lengths: int32 [512], P('dev'), may hold values from 2 to 256, as said below
Outputs:
- new_latent: bfloat16 [512, 576], P('dev')
- context: bfloat16 [512, 128, 512], P('dev', 'role')
Inputs may be any that keep to these rules, and one draw needn't show every extreme that they name: `lengths`: one request has exactly 256 live positions.
All inputs are finite; a program needn't handle non-finite values.
Results may differ from a plain program's by a relative error of at most 0.0063.
Values may be sent and summed in bfloat16 or wider, within the bound.
A program may use at most 128 MiB of HBM per device.

v0:
```python
import jax
import jax.numpy as jnp
from jax import lax
from jax.sharding import PartitionSpec as P

EXPERTS = 16


score_scale = 192.0 ** (-0.5)
norm_eps = 1e-06


def partner_2(block, axis, stride):
    count = lax.axis_size(axis)
    route = []
    for low in range(count):
        high = low | 1 << stride
        if high != low and high < count:
            route += [(low, high), (high, low)]
    return lax.ppermute(block, axis, route)


def rms_scale(values, gain):
    mean_square = jnp.mean(jnp.square(values), axis=-1, keepdims=True)
    return values * lax.rsqrt(mean_square + norm_eps) * gain


def expert_block(received, w_gate, w_up, w_down, working):
    sources, slot_count, feature_width = received.shape
    flat_rows = received.reshape(sources * slot_count, feature_width)

    def compute(rows_in):
        gate_act = jnp.dot(rows_in, w_gate, preferred_element_type=jnp.float32)
        up_act = jnp.dot(rows_in, w_up, preferred_element_type=jnp.float32)
        hidden_act = (jax.nn.silu(gate_act) * up_act).astype(jnp.bfloat16)
        return jnp.dot(hidden_act, w_down, preferred_element_type=jnp.float32).astype(jnp.bfloat16)

    def skipped(rows_in):
        return jnp.zeros_like(rows_in)

    produced = lax.cond(working, compute, skipped, flat_rows)
    return produced.reshape(sources, slot_count, feature_width)


def moe_latent(
    own_rows,
    own_ids,
    own_gates,
    working,
    ffn_gain,
    w_gate,
    w_up,
    w_down,
    attn_gain,
    w_latent,
    kv_gain,
):
    devices = lax.axis_size("dev")
    shards_per_expert = devices // EXPERTS
    normed = rms_scale(own_rows.astype(jnp.float32), ffn_gain).astype(jnp.bfloat16)
    expert_of = jnp.arange(devices, dtype=jnp.int32) // shards_per_expert
    matches = own_ids[:, :, None] == expert_of[None, None, :]
    weight_dev = jnp.sum(jnp.where(matches, own_gates[:, :, None], 0.0), axis=1)
    routed = jnp.any(matches, axis=1)
    routed = jnp.logical_and(routed, working)
    outgoing = jnp.where(routed.T[:, :, None], normed[None, :, :], jnp.zeros((), jnp.bfloat16))
    produced = expert_block(
        lax.all_to_all(outgoing, "dev", split_axis=0, concat_axis=0, tiled=True),
        w_gate,
        w_up,
        w_down,
        working,
    )
    returned = lax.all_to_all(produced, "dev", split_axis=0, concat_axis=0, tiled=True)
    combined = jnp.sum(weight_dev.T[:, :, None] * returned.astype(jnp.float32), axis=0)
    residual = lax.optimization_barrier(
        (own_rows.astype(jnp.float32) + combined).astype(jnp.bfloat16)
    )
    attn_in = rms_scale(residual.astype(jnp.float32), attn_gain).astype(jnp.bfloat16)
    spread = lax.all_to_all(attn_in, "dev", split_axis=1, concat_axis=0, tiled=True)
    compressed = lax.psum_scatter(
        jnp.dot(spread, w_latent, preferred_element_type=jnp.float32),
        "dev",
        scatter_dimension=0,
        tiled=True,
    )
    latent = kv_gain.shape[0]
    content = rms_scale(compressed[:, :latent], kv_gain)
    return jnp.concatenate([content, compressed[:, latent:]], axis=1).astype(jnp.bfloat16)


def cache_state(query_part, cache, lengths, latent):
    scores = (
        jnp.einsum("rhc,rlc->rhl", query_part, cache, preferred_element_type=jnp.float32)
        * score_scale
    )
    live_mask = jnp.arange(cache.shape[1], dtype=jnp.int32)[None, None, :] < lengths[:, None, None]
    scores = jnp.where(live_mask, scores, -jnp.inf)
    peak_cache = jnp.max(scores, axis=2)
    weights = jnp.where(live_mask, jnp.exp(scores - peak_cache[:, :, None]), 0.0).astype(
        jnp.bfloat16
    )
    weight_sum = jnp.sum(weights.astype(jnp.float32), axis=2)
    summed = jnp.einsum(
        "rhl,rlc->rhc", weights, cache[:, :, :latent], preferred_element_type=jnp.float32
    )
    return (peak_cache, weight_sum, summed)


def finish(peak_cache, weight_sum, summed, query_part, latent_rows, latent):
    new_score = (
        jnp.einsum("rhc,rc->rh", query_part, latent_rows, preferred_element_type=jnp.float32)
        * score_scale
    )
    joint_peak = jnp.maximum(peak_cache, new_score)
    old_scale = jnp.exp(peak_cache - joint_peak)
    new_scale = jnp.exp(new_score - joint_peak)
    values = latent_rows[:, None, :latent].astype(jnp.float32)
    merged = (old_scale[:, :, None] * summed + new_scale[:, :, None] * values) / (
        old_scale * weight_sum + new_scale
    )[:, :, None]
    return merged.astype(jnp.bfloat16)


def shards(
    hidden_in,
    expert_ids,
    gate_values,
    ffn_gain,
    w_gate,
    w_up,
    w_down,
    attn_gain,
    w_latent,
    kv_gain,
    queries,
    cache,
    lengths,
):
    role_index = lax.axis_index("role")
    is_first = role_index == 0
    latent = kv_gain.shape[0]
    head_count = queries.shape[1] // 2
    head_queries = lax.dynamic_slice_in_dim(queries, role_index * head_count, head_count, 1)
    is_expert = role_index == 1
    own_latent = moe_latent(
        hidden_in,
        expert_ids,
        gate_values,
        is_expert,
        ffn_gain,
        w_gate,
        w_up,
        w_down,
        attn_gain,
        w_latent,
        kv_gain,
    )

    def attend():
        return cache_state(queries, cache, lengths, latent)

    def resting():
        row_total = queries.shape[0]
        all_heads = queries.shape[1]
        return (
            jnp.zeros((row_total, all_heads), jnp.float32),
            jnp.zeros((row_total, all_heads), jnp.float32),
            jnp.zeros((row_total, all_heads, latent), jnp.float32),
        )

    peak_all, sum_all, summed_all = lax.cond(is_first, attend, resting)
    partner = partner_2(
        (
            peak_all[:, head_count:],
            sum_all[:, head_count:],
            summed_all[:, head_count:],
            own_latent.astype(jnp.float32),
        ),
        "role",
        0,
    )
    peak_cache = jnp.where(is_first, peak_all[:, :head_count], partner[0])
    weight_sum = jnp.where(is_first, sum_all[:, :head_count], partner[1])
    summed = jnp.where(is_first, summed_all[:, :head_count], partner[2])
    new_latent = jnp.where(is_first, partner[3].astype(jnp.bfloat16), own_latent)
    context = finish(peak_cache, weight_sum, summed, head_queries, new_latent, latent)
    return (new_latent, context)


def solution(mesh):
    in_specs = (
        P("dev", None),
        P("dev", None),
        P("dev", None),
        P(),
        P(None, "dev"),
        P(None, "dev"),
        P("dev", None),
        P(),
        P("dev", None),
        P(),
        P("dev", None, None),
        P("dev", None, None),
        P("dev"),
    )
    out_specs = (P("dev", None), P("dev", "role", None))
    return jax.shard_map(shards, mesh=mesh, in_specs=in_specs, out_specs=out_specs, check_vma=False)
```

profile of v0, /device:TPU:1, one launch (start us, length us, event | category | flops | bytes accessed | tf_op | source)
XLA Modules:
  0.0 403.6 jit_solution(11789397365605181997)
XLA Ops:
  7.2 0.8 compare_reduce_fusion
  8.1 1.1 fusion.28
  9.2 1.0 fusion.30
  10.2 3.6 broadcast_select_fusion
  13.8 12.2 %all-to-all-start = ((bf16[64,8,7168]{2,1,0:T(8,128)(2,1)}), bf16[64,8,7168]{2,1,0:T(8,128)(2,1)}, u32[]{:S(2)}, u32[]{:S(2)}) async-start(bf16[64,8,7168]{2,1,0:T(8,128)(2,1)} %broadcast_select_fusion), calls=%async_computation | async-start | bytes 14680064 | tf_op jit(solution)/shard_map/all_to_all | solution.py:68
  26.0 97.5 %all-to-all-done = bf16[64,8,7168]{2,1,0:T(8,128)(2,1)} async-done(((bf16[64,8,7168]{2,1,0:T(8,128)(2,1)}), bf16[64,8,7168]{2,1,0:T(8,128)(2,1)}, u32[]{:S(2)}, u32[]{:S(2)}) %all-to-all-start) | async-done | bytes 7340064 | tf_op jit(solution)/shard_map/all_to_all | solution.py:68
  123.5 24.8 %conditional.2 = (bf16[512,7168]{1,0:T(8,128)(2,1)}) conditional(s32[]{:T(128)} %convert_element_type.52, () %tuple.22, (bf16[64,8,7168]{2,1,0:T(8,128)(2,1)}, bf16[7168,512]{1,0:T(8,128)(2,1)}, bf16[7168,512]{1,0:T(8,128)(2,1)}, bf16[512,7168]{1,0:T(8,128)(2,1)}) %tuple.23), branch_computations={%region_3.4_spmd, %region_4.5_spmd} | conditional | flops 11279532032 | bytes 46137352 | solution.py:41
  123.5 8.4 %fusion.2 = f32[512,512]{1,0:T(8,128)S(1)} fusion(bf16[7168,512]{1,0:T(8,128)(2,1)} %get-tuple-element.36, bf16[64,8,7168]{2,1,0:T(8,128)(2,1)} %get-tuple-element.18), kind=kOutput, calls=%fused_computation.3 | convolution fusion | flops 3758096384 | bytes 15728640 | tf_op jit(solution)/shard_map/cond/branch_1_fun/dot_general | solution.py:33
  132.0 16.4 %convolution_convert_fusion = bf16[512,7168]{1,0:T(8,128)(2,1)} fusion(bf16[512,7168]{1,0:T(8,128)(2,1)} %get-tuple-element.38, bf16[7168,512]{1,0:T(8,128)(2,1)} %get-tuple-element.37, bf16[64,8,7168]{2,1,0:T(8,128)(2,1)} %get-tuple-element.18, f32[512,512]{1,0:T(8,128)S(1)} %fusion.2), kind=kOutput, calls=%fused_computation | convolution fusion | flops 7521435648 | bytes 30408704 | tf_op jit(solution)/shard_map/cond/branch_1_fun/dot_general | solution.py:36
  148.3 12.5 %all-to-all-start.1 = ((bf16[64,8,7168]{2,1,0:T(8,128)(2,1)}), bf16[64,8,7168]{2,1,0:T(8,128)(2,1)}, u32[]{:S(2)}, u32[]{:S(2)}) async-start(bf16[64,8,7168]{2,1,0:T(8,128)(2,1)} %bitcast.30), calls=%async_computation.1 | async-start | bytes 14680064 | tf_op jit(solution)/shard_map/all_to_all | solution.py:74
  161.1 77.4 %all-to-all-done.1 = bf16[64,8,7168]{2,1,0:T(8,128)(2,1)} async-done(((bf16[64,8,7168]{2,1,0:T(8,128)(2,1)}), bf16[64,8,7168]{2,1,0:T(8,128)(2,1)}, u32[]{:S(2)}, u32[]{:S(2)}) %all-to-all-start.1) | async-done | bytes 7340064 | tf_op jit(solution)/shard_map/all_to_all | solution.py:74
  238.5 4.8 %multiply_reduce_fusion = f32[8,7168]{1,0:T(8,128)S(1)} fusion(bf16[64,8,7168]{2,1,0:T(8,128)(2,1)} %all-to-all-done.1, f32[64,8]{1,0:T(8,128)S(1)} %copy.29), kind=kLoop, calls=%fused_computation.22 | loop fusion | flops 10952704 | bytes 7571456 | tf_op jit(solution)/shard_map/reduce_sum | solution.py:75
  243.4 0.2 fusion.25
  243.7 0.2 all_to_all.22
  244.0 15.5 %all_to_all.29 = bf16[8,64,112]{2,0,1:T(8,128)(2,1)S(1)} all-to-all(bf16[8,64,112]{2,0,1:T(8,128)(2,1)S(1)} %copy.31), channel_id=1, replica_groups=mesh['role'=2,'dev'=64] {'dev'}, dimensions={1} | all-to-all | bytes 229376 | tf_op jit(solution)/shard_map/all_to_all | solution.py:80
  259.5 1.4 fusion.32
  261.0 2.2 conditional.3
  261.0 1.6 broadcast.110
  262.6 0.6 broadcast.109
  263.2 1.3 slice.36
  264.5 7.2 %collective-permute-start.2 = (f32[8,64,512]{2,1,0:T(8,128)S(1)}, f32[8,64,512]{2,1,0:T(8,128)S(1)}, u32[]{:S(2)}, u32[]{:S(2)}) collective-permute-start(f32[8,64,512]{2,1,0:T(8,128)S(1)} %slice.36), channel_id=1, source_target_pairs={{0,64},{64,0},{1,65},{65,1},{2,66},{66,2},{3,67},{67,3},{4,68},{68... | collective-permute-start | bytes 3145736 | tf_op jit(solution)/shard_map/ppermute | solution.py:20
  271.7 1.2 dynamic-slice
  273.6 111.7 %all-reduce.3.cloned.1.call-done = f32[512,576]{1,0:T(8,128)} async-done(((f32[512,576]{1,0:T(8,128)}), f32[512,576]{1,0:T(8,128)}) %all-reduce.3.cloned.1.call-update) | async-done | bytes 1179664
  385.3 0.8 multiply_reduce_fusion.1
  386.2 0.8 multiply_convert_fusion
  387.0 0.8 dynamic-slice.7
  387.7 2.7 collective-permute-start
  390.5 0.8 slice.34
  391.3 0.5 collective-permute-start.3
  391.9 1.8 fusion.23
  393.6 0.7 multiply_add_fusion
  394.3 2.4 divide_convert_fusion
  (39 shorter events, 0.8 us)
Async XLA Ops:
  7.2 252.3 %copy-start = (bf16[112,576]{1,0:T(8,128)(2,1)S(1)}, bf16[112,576]{1,0:T(8,128)(2,1)}, u32[]{:S(2)}) copy-start(bf16[112,576]{1,0:T(8,128)(2,1)} %param.25) | copy-start | bytes 387076
  13.8 109.7 %all-to-all-start = ((bf16[64,8,7168]{2,1,0:T(8,128)(2,1)}), bf16[64,8,7168]{2,1,0:T(8,128)(2,1)}, u32[]{:S(2)}, u32[]{:S(2)}) async-start(bf16[64,8,7168]{2,1,0:T(8,128)(2,1)} %broadcast_select_fusion), calls=%async_computation | async-start | bytes 14680064 | tf_op jit(solution)/shard_map/all_to_all | solution.py:68
  148.3 12.6 %copy-start.6 = (s32[8,8]{1,0:T(8,128)S(1)}, s32[8,8]{1,0:T(8,128)}, u32[]{:S(2)}) copy-start(s32[8,8]{1,0:T(8,128)} %param.18) | copy-start | bytes 772
  148.3 12.6 %copy-start.7 = (f32[8,8]{1,0:T(8,128)S(1)}, f32[8,8]{1,0:T(8,128)}, u32[]{:S(2)}) copy-start(f32[8,8]{1,0:T(8,128)} %param.19) | copy-start | bytes 772
  148.3 90.2 %all-to-all-start.1 = ((bf16[64,8,7168]{2,1,0:T(8,128)(2,1)}), bf16[64,8,7168]{2,1,0:T(8,128)(2,1)}, u32[]{:S(2)}, u32[]{:S(2)}) async-start(bf16[64,8,7168]{2,1,0:T(8,128)(2,1)} %bitcast.30), calls=%async_computation.1 | async-start | bytes 14680064 | tf_op jit(solution)/shard_map/all_to_all | solution.py:74
  160.8 82.5 %copy-start.2 = (bf16[8,7168]{1,0:T(8,128)(2,1)S(1)}, bf16[8,7168]{1,0:T(8,128)(2,1)}, u32[]{:S(2)}) copy-start(bf16[8,7168]{1,0:T(8,128)(2,1)} %param.17) | copy-start | bytes 344068
  160.8 82.7 %copy-start.5 = (f32[7168]{0:T(1024)S(1)}, f32[7168]{0:T(1024)}, u32[]{:S(2)}) copy-start(f32[7168]{0:T(1024)} %param.24) | copy-start | bytes 86020
  160.9 100.1 %copy-start.1 = (bf16[8,256,576]{1,2,0:T(8,128)(2,1)S(1)}, bf16[8,256,576]{1,2,0:T(8,128)(2,1)}, u32[]{:S(2)}) copy-start(bf16[8,256,576]{1,2,0:T(8,128)(2,1)} %param.28) | copy-start | bytes 7077892
  160.9 100.1 %copy-start.8 = (s32[8]{0:T(128)S(1)}, s32[8]{0:T(128)}, u32[]{:S(2)}) copy-start(s32[8]{0:T(128)} %param.29) | copy-start | bytes 100
  160.9 224.4 %all-reduce.3.cloned.1.call-start = ((), (), s32[]{:S(2)}) async-start(), calls=%async_computation.3 | async-start | bytes 2621440
  264.5 129.8 %collective-permute-start.2 = (f32[8,64,512]{2,1,0:T(8,128)S(1)}, f32[8,64,512]{2,1,0:T(8,128)S(1)}, u32[]{:S(2)}, u32[]{:S(2)}) collective-permute-start(f32[8,64,512]{2,1,0:T(8,128)S(1)} %slice.36), channel_id=1, source_target_pairs={{0,64},{64,0},{1,65},{65,1},{2,66},{66,2},{3,67},{67,3},{4,68},{68... | collective-permute-start | bytes 3145736 | tf_op jit(solution)/shard_map/ppermute | solution.py:20
  387.7 4.1 %collective-permute-start = (bf16[8,576]{1,0:T(8,128)(2,1)S(1)}, bf16[8,576]{1,0:T(8,128)(2,1)S(1)}, u32[]{:S(2)}, u32[]{:S(2)}) collective-permute-start(bf16[8,576]{1,0:T(8,128)(2,1)S(1)} %fusion.36), channel_id=1, source_target_pairs={{0,64},{64,0},{1,65},{65,1},{2,66},{66,2},{3,67},{67,3},{4,68},{68... | collective-permute-start | bytes 27656 | tf_op jit(solution)/shard_map/ppermute | solution.py:20
  391.2 2.4 collective-permute-start.1
  391.3 2.3 collective-permute-start.3
  391.8 4.9 %copy-start.3 = (bf16[8,576]{1,0:T(8,128)(2,1)}, bf16[8,576]{1,0:T(8,128)(2,1)S(1)}, u32[]{:S(2)}) copy-start(bf16[8,576]{1,0:T(8,128)(2,1)S(1)} %convert_select_fusion) | copy-start | bytes 27652
Sparse Core Ops, SparseCore 0:
  261.1 124.2 all-reduce.2
where the time goes:
time: 404 us
  waiting for transfers between devices  287 us (71%)
  starting transfers between devices  35.2 us (9%)
  matrix products  28 us (7%)
  other arithmetic  16.4 us (4%)
  blocking collectives  15.5 us (4%)
  between operations  14.9 us (4%)
  local copies, waits for them, and re-layouts  6.84 us (2%)
    unnamed x2, waiting for transfers between devices  112 us
    all_to_all x1, waiting for transfers between devices, moe_latent(): lax.all_to_all(outgoing, 'dev', split_axis=0, concat_axis=0, tiled=True)  97.5 us
    all_to_all x1, waiting for transfers between devices, moe_latent(): lax.all_to_all(produced, 'dev', split_axis=0, concat_axis=0, tiled=True)  77.4 us
    dot_general x1, matrix products, compute(): jnp.dot(hidden_act, w_down, preferred_element_type=jnp.float32)  16.4 us
    all_to_all x1, blocking collectives, moe_latent(): lax.all_to_all(attn_in, 'dev', split_axis=1, concat_axis=0, tiled=True)  15.5 us
    all_to_all x1, starting transfers between devices, moe_latent(): lax.all_to_all(produced, 'dev', split_axis=0, concat_axis=0, tiled=True)  12.5 us
    all_to_all x1, starting transfers between devices, moe_latent(): lax.all_to_all(outgoing, 'dev', split_axis=0, concat_axis=0, tiled=True)  12.2 us
    ppermute x4, starting transfers between devices, partner_2(): return lax.ppermute(block, axis, route)  10.5 us
  transfers between devices with their start and end apart: 7, of which 3 were waited for; matrix products, arithmetic and copies ran while one was open for 3% of the time, Pallas kernels for 0%

commit v1 on v0

v1 whole, which is shorter than its diff:
```python
import jax
import jax.numpy as jnp
from jax import lax
from jax.experimental import pallas as pl
from jax.experimental.pallas import tpu as pltpu
from jax.sharding import PartitionSpec as P

MESH = pl.DeviceIdType.MESH
F32 = jnp.float32
BF16 = jnp.bfloat16

SCORE_SCALE = 192.0 ** (-0.5)
EPS = 1e-06
D = 7168
SLICE = 1792
FFD = 512
LAT = 512
KVW = 576
EXPERTS = 16
WIDTH = (640, 640, 512)
OFF = (0, 640, 1280)
GATHER = (("x", "y", "z"), ("y", "z", "x"), ("z", "x", "y"))
SCATTER = tuple(order[::-1] for order in GATHER)
DIM = {"z": 0, "x": 1, "y": 2}
LOW_ROWS = 64


def kernel(
    hidden,
    ids,
    gates,
    ffn_gain,
    attn_gain,
    kv_gain,
    lengths,
    w_gate,
    w_up,
    w_down,
    w_latent,
    queries,
    cache,
    new_latent,
    context,
    wg,
    wu,
    wd,
    wl,
    qv,
    cv,
    summed,
    peaks,
    sums,
    xh,
    xe,
    yh,
    ye,
    hid16,
    ga,
    gb,
    gc,
    acc_g,
    acc_u,
    gate_col,
    act,
    oa,
    ob,
    oc,
    rs_bufs,
    att,
    tbuf,
    ebuf,
    send_sems,
    recv_sems,
    load_sems,
):
    role = lax.axis_index("role")
    dev = lax.axis_index("dev")
    z, y, x = dev // 16, lax.rem(dev // 4, 4), lax.rem(dev, 4)
    at = {"z": z, "y": y, "x": x}
    stride = {"z": 16, "y": 4, "x": 1}

    def plus(axis, d):
        return lax.rem(at[axis] + (d + 4), 4)

    def near(axis, d):
        return dev + (plus(axis, d) - at[axis]) * stride[axis]

    count = [0]
    sent = []

    def remote(src, dst, to_dev, to_role=None):
        i = count[0]
        count[0] += 1
        return pltpu.make_async_remote_copy(
            src_ref=src,
            dst_ref=dst,
            send_sem=send_sems.at[i],
            recv_sem=recv_sems.at[i],
            device_id=(role if to_role is None else to_role, to_dev),
            device_id_type=MESH,
        )

    def go(copy):
        copy.start()
        sent.append(copy)
        return copy

    loads = []

    def load(src, dst):
        copy = pltpu.make_async_copy(src, dst, load_sems.at[len(loads)])
        copy.start()
        loads.append(copy)
        return copy

    load_q = load(queries.at[:, pl.ds(pl.multiple_of(role * 64, 64), 64), :], qv)
    load_c = load(cache, cv)
    load_g = [load(w_gate.at[pl.ds(i * SLICE, SLICE)], wg.at[pl.ds(i * SLICE, SLICE)]) for i in range(4)]
    load_u = [load(w_up.at[pl.ds(i * SLICE, SLICE)], wu.at[pl.ds(i * SLICE, SLICE)]) for i in range(4)]
    load_d = [load(w_down.at[pl.ds(i * 128, 128)], wd.at[pl.ds(i * 128, 128)]) for i in range(4)]

    barrier = pltpu.get_barrier_semaphore()
    partners = [(role, near(axis, d)) for axis in "xyz" for d in (1, 2, 3)]
    partners += [(1 - role, near("z", d)) for d in (0, 1, 2, 3)]
    for partner in partners:
        pl.semaphore_signal(barrier, inc=1, device_id=partner, device_id_type=MESH)

    hid = hidden[...].astype(F32)
    scale = lax.rsqrt(jnp.mean(jnp.square(hid), axis=-1, keepdims=True) + EPS)
    lane = lax.broadcasted_iota(jnp.int32, (8, 128), 1)
    table = jnp.zeros((8, 128), F32)
    for k in range(8):
        table = jnp.where(ids[:, k : k + 1] == lane % EXPERTS, gates[:, k : k + 1], table)
    extra = jnp.where(lane < 2 * EXPERTS, table, scale)
    own = jnp.where(role == 0, hid[0:4], hid[4:8])
    for i in range(4):
        xh[i] = own[:, i * SLICE : (i + 1) * SLICE].astype(BF16)
    xe[...] = jnp.where(role == 0, extra[0:4], extra[4:8])

    pl.semaphore_wait(barrier, len(partners))

    first = []
    for d in (2, 1, 3):
        first.append(go(remote(xh.at[plus("z", d)], yh.at[z], near("z", d))))
        first.append(go(remote(xe, ye.at[z], near("z", d))))

    def latent_copies():
        out = []
        for r, rows, axes in ((0, pl.ds(0, LOW_ROWS), "xy"), (1, pl.ds(LOW_ROWS, 112 - LOW_ROWS), "yx")):
            a, b = axes
            base = count[0]
            one = [
                remote(
                    wl.at[y, x, rows],
                    wl.at[y, x, rows],
                    near(a, d),
                )
                for d in (2, 1, 3)
            ]

            def place(pos, half, a=a, rows=rows):
                full = pl.ds(0, 4) if half is None else pl.ds(2 * half, 2)
                return wl.at[pos, full, rows] if a == "x" else wl.at[full, pos, rows]

            two = [remote(place(at[b], None), place(at[b], None), near(b, d)) for d in (1, 3)]
            three = [
                remote(place(plus(b, -1), 0), place(plus(b, -1), 0), near(b, 1)),
                remote(place(plus(b, 1), 1), place(plus(b, 1), 1), near(b, 3)),
            ]
            share = remote(wl.at[:, :, rows], wl.at[:, :, rows], dev, 1 - role)
            out.append((r, one, two, three, share))
            if r == 0:
                count[0] = base
        return out

    latent_plan = latent_copies()

    def latent_step(action):
        for r, one, two, three, share in latent_plan:

            @pl.when(role == r)
            def _(one=one, two=two, three=three, share=share):
                action(one, two, three, share)

    for r, rows in ((0, pl.ds(0, LOW_ROWS)), (1, pl.ds(LOW_ROWS, 112 - LOW_ROWS))):

        @pl.when(role == r)
        def _(rows=rows):
            own_rows = pltpu.make_async_copy(w_latent.at[rows], wl.at[y, x, rows], load_sems.at[15])
            own_rows.start()
            own_rows.wait()

    latent_step(lambda one, two, three, share: [c.start() for c in one])

    for copy in first:
        copy.wait_recv()
    yh[z] = xh[z]
    ye[z] = xe[...]
    h16 = jnp.concatenate([yh[i].astype(F32) for i in range(4)], axis=0)
    e16 = jnp.concatenate([ye[i] for i in range(4)], axis=0)
    hid16[...] = h16
    col = pl.ds(pl.multiple_of(z * SLICE, 128), SLICE)
    normed = (h16 * e16[:, 2 * EXPERTS : 2 * EXPERTS + 1] * ffn_gain[:, col]).astype(BF16)
    ga[z, x, y] = normed[:, 0:640]
    gb[z, x, y] = normed[:, 640:1280]
    gc[z, x, y, :, 0:512] = normed[:, 1280:1792]
    lane16 = lax.broadcasted_iota(jnp.int32, (16, 128), 1)
    high = e16.astype(BF16).astype(F32)
    gc[z, x, y, :, 512:640] = jnp.where(lane16 < EXPERTS, high, e16 - high).astype(BF16)

    gathered = (ga, gb, gc)

    def spot(order, k, value, half=None):
        spec = {}
        for axis in order[:k]:
            spec[axis] = pl.ds(0, 4)
        if half is not None:
            spec[order[0]] = pl.ds(2 * half, 2)
        spec[order[k]] = value
        for axis in order[k + 1 :]:
            spec[axis] = at[axis]
        return spec["z"], spec["x"], spec["y"]

    gstate = [None] * 3

    def gather_start(p, k):
        order, ref = GATHER[p], gathered[p]
        a = order[k]
        here = ref.at[spot(order, k, at[a])]
        copies = [go(remote(here, here, near(a, d))) for d in ((1, 3) if k else (2, 1, 3))]
        gstate[p] = copies

    def gather_forward(p, k):
        order, ref = GATHER[p], gathered[p]
        a = order[k]
        right, left = gstate[p]
        right.wait_recv()
        one = ref.at[spot(order, k, plus(a, -1), 0)]
        one = go(remote(one, one, near(a, 1)))
        left.wait_recv()
        two = ref.at[spot(order, k, plus(a, 1), 1)]
        two = go(remote(two, two, near(a, 3)))
        gstate[p] = [one, two]

    def gather_finish(p):
        for copy in gstate[p]:
            copy.wait_recv()

    def attend(lo, hi):
        @pl.loop(lo, hi)
        def _(i):
            s = lax.dot_general(qv[i], cv[i], (((1,), (1,)), ((), ())), preferred_element_type=F32)
            s = s * SCORE_SCALE
            live = lax.broadcasted_iota(jnp.int32, (64, 256), 1) < lengths[i]
            s = jnp.where(live, s, -jnp.inf)
            peak = jnp.max(s, axis=1, keepdims=True)
            w = jnp.where(live, jnp.exp(s - peak), 0.0).astype(BF16)
            sums[i] = jnp.broadcast_to(jnp.sum(w.astype(F32), axis=1, keepdims=True), (64, 128))
            peaks[i] = jnp.broadcast_to(peak, (64, 128))
            summed[i] = jnp.dot(w, cv[i, :, 0:LAT], preferred_element_type=F32)

    def gate_up(p, zz):
        rows = gathered[p][zz].reshape(256, 640)
        if p == 2:
            rows = rows[:, 0:512]
        k = pl.ds(pl.multiple_of(zz * SLICE + OFF[p], 128), WIDTH[p])
        acc_g[...] += jnp.dot(rows, wg[k, :], preferred_element_type=F32)
        acc_u[...] += jnp.dot(rows, wu[k, :], preferred_element_type=F32)

    for p in range(3):
        gather_start(p, 0)
    load_q.wait()
    load_c.wait()
    for p in range(3):
        gather_finish(p)
        gather_start(p, 1)
    attend(0, 4)
    for p in range(3):
        gather_forward(p, 1)
    attend(4, 8)
    for p in range(3):
        gather_finish(p)
        gather_start(p, 2)
    latent_step(lambda one, two, three, share: [c.wait_recv() for c in one])
    for copy in load_g + load_u:
        copy.wait()
    acc_g[...] = jnp.zeros_like(acc_g)
    acc_u[...] = jnp.zeros_like(acc_u)
    gate_up(0, z)
    for p in range(3):
        gather_forward(p, 2)
    latent_step(lambda one, two, three, share: [c.start() for c in two])
    gate_up(0, plus("z", 1))
    gate_up(0, plus("z", 3))
    for p in range(3):
        gather_finish(p)
    gate_up(0, plus("z", 2))
    for p in (1, 2):

        @pl.loop(0, 4)
        def _(zz, p=p):
            gate_up(p, zz)

    expert = z * 4 + y
    mine = lax.broadcasted_iota(jnp.int32, (256, 128), 1)
    mine = jnp.logical_or(mine == expert, mine == expert + EXPERTS)
    table_all = gc[0, :, :, :, 512:640].reshape(256, 128).astype(F32)
    gate_col[...] = jnp.sum(jnp.where(mine, table_all, 0.0), axis=1, keepdims=True)

    @pl.loop(0, 16)
    def _(i):
        rows = pl.ds(pl.multiple_of(i * 16, 16), 16)
        g = acc_g[rows, :]
        act[rows, :] = (g / (1.0 + jnp.exp(-g)) * acc_u[rows, :] * gate_col[rows, :]).astype(BF16)

    for copy in load_d:
        copy.wait()
    latent_step(
        lambda one, two, three, share: [
            two[0].wait_recv(),
            three[0].start(),
            two[1].wait_recv(),
            three[1].start(),
        ]
    )

    outs = (oa, ob, oc)

    def down(p, zz):
        k = pl.ds(pl.multiple_of(zz * SLICE + OFF[p], 128), WIDTH[p])
        out = jnp.dot(act[...], wd[:, k], preferred_element_type=F32)
        outs[p][zz] = out.astype(BF16).reshape(4, 4, 16, WIDTH[p])

    def block(order, s, value, half=None):
        spec = {}
        for axis in order[:s]:
            spec[axis] = pl.ds(0, 1)
        spec[order[s]] = pl.ds(value, 1)
        for axis in order[s + 1 :]:
            spec[axis] = pl.ds(0, 4)
        if half is not None:
            spec[order[2]] = pl.ds(2 * half, 2)
        return spec["z"], spec["x"], spec["y"]

    def part_of(order, half):
        spec = {axis: slice(None) for axis in order}
        spec[order[2]] = pl.ds(2 * half, 2)
        return spec["z"], spec["x"], spec["y"]

    sstate = [None] * 3

    def scatter_opposite(p, s, cur):
        order = SCATTER[p]
        b = order[s]
        fl, fr, rl, rr, out = rs_bufs[p][s]
        one = go(remote(cur.at[block(order, s, plus(b, 2), 0)], fl, near(b, 1)))
        two = go(remote(cur.at[block(order, s, plus(b, 2), 1)], fr, near(b, 3)))
        sstate[p] = [one, two]

    def scatter_direct(p, s, cur):
        order = SCATTER[p]
        b = order[s]
        fl, fr, rl, rr, out = rs_bufs[p][s]
        one = go(remote(cur.at[block(order, s, plus(b, 1), 1)], rl.at[part_of(order, 1)], near(b, 1)))
        two = go(remote(cur.at[block(order, s, plus(b, 3), 0)], rr.at[part_of(order, 0)], near(b, 3)))
        sstate[p] += [one, two]

    def add_into(dst, pieces):
        total = pieces[0].astype(F32)
        for piece in pieces[1:]:
            total = total + piece.astype(F32)
        dst[...] = total.astype(BF16)

    def scatter_forward(p, s, cur):
        order = SCATTER[p]
        b = order[s]
        fl, fr, rl, rr, out = rs_bufs[p][s]
        one, two, three, four = sstate[p]
        one.wait_recv()
        add_into(fl, [fl[...], cur[block(order, s, plus(b, 1), 0)]])
        one = go(remote(fl, rl.at[part_of(order, 0)], near(b, 1)))
        two.wait_recv()
        add_into(fr, [fr[...], cur[block(order, s, plus(b, 3), 1)]])
        two = go(remote(fr, rr.at[part_of(order, 1)], near(b, 3)))
        sstate[p] = [three, four, one, two]

    def scatter_finish(p, s, cur):
        order = SCATTER[p]
        b = order[s]
        fl, fr, rl, rr, out = rs_bufs[p][s]
        for copy in sstate[p]:
            copy.wait_recv()
        add_into(out, [cur[block(order, s, at[b])], rl[...], rr[...]])
        return out

    down(0, plus("z", 2))
    scatter_opposite(0, 0, oa)
    down(0, plus("z", 1))
    down(0, plus("z", 3))
    scatter_direct(0, 0, oa)
    for p in (1, 2):

        @pl.loop(0, 4)
        def _(zz, p=p):
            down(p, zz)

        scatter_opposite(p, 0, outs[p])
        scatter_direct(p, 0, outs[p])
    down(0, z)
    cur = list(outs)
    for p in range(3):
        scatter_forward(p, 0, cur[p])
    latent_step(lambda one, two, three, share: [three[0].wait_recv(), three[1].wait_recv(), share.start()])
    for s in (0, 1):
        for p in range(3):
            cur[p] = scatter_finish(p, s, cur[p])
            if s == 0:
                scatter_opposite(p, 1, cur[p])
                scatter_direct(p, 1, cur[p])
            else:
                order = SCATTER[p]
                b = order[2]
                slots = rs_bufs[p][2]
                sstate[p] = [
                    go(remote(cur[p].at[block(order, 2, plus(b, d))], slots.at[d - 1], near(b, d))) for d in (2, 1, 3)
                ]
        if s == 0:
            for p in range(3):
                scatter_forward(p, 1, cur[p])

    squares = jnp.zeros((16, 1), F32)
    for p in range(3):
        order = SCATTER[p]
        for copy in sstate[p]:
            copy.wait_recv()
        total = cur[p][block(order, 2, at[order[2]])].reshape(16, WIDTH[p]).astype(F32)
        for d in range(3):
            total = total + rs_bufs[p][2][d].reshape(16, WIDTH[p]).astype(F32)
        cols = slice(OFF[p], OFF[p] + WIDTH[p])
        residual = (hid16[:, cols] + total).astype(BF16).astype(F32)
        squares = squares + jnp.sum(jnp.square(residual), axis=1, keepdims=True)
        gain = attn_gain[:, pl.ds(pl.multiple_of(z * SLICE + OFF[p], 128), WIDTH[p])]
        att[:, cols] = (residual * gain).astype(BF16)
    for r, one, two, three, share in latent_plan:

        @pl.when(role == r)
        def _(r=r):
            rows = pl.ds(LOW_ROWS, 112 - LOW_ROWS) if r == 0 else pl.ds(0, LOW_ROWS)
            pltpu.make_async_remote_copy(
                src_ref=wl.at[:, :, rows],
                dst_ref=wl.at[:, :, rows],
                send_sem=send_sems.at[share_at],
                recv_sem=recv_sems.at[share_at],
                device_id=(1 - role, dev),
                device_id_type=MESH,
            ).wait_recv()

    partial = jnp.dot(att[...], wl[...].reshape(SLICE, KVW), preferred_element_type=F32)
    partial = jnp.concatenate([partial, jnp.broadcast_to(squares, (16, 64))], axis=1)
    for i in range(4):
        tbuf[i] = partial[4 * i : 4 * i + 4]

    last = []
    for d in (2, 1, 3, 0):
        for other in (0, 1):
            if d == 0 and other == 0:
                continue
            to_role = 1 - role if other else role
            last.append(go(remote(tbuf.at[plus("z", d)], ebuf.at[z, role], near("z", d), to_role)))
    ebuf[z, role] = tbuf[z]
    for copy in last:
        copy.wait_recv()
    halves = []
    for r in range(2):
        total = ebuf[0, r]
        for i in range(1, 4):
            total = total + ebuf[i, r]
        halves.append(total)
    comp = jnp.concatenate(halves, axis=0)
    comp = comp[:, 0:KVW] * lax.rsqrt(comp[:, KVW : KVW + 1] / D + EPS)
    content = comp[:, 0:LAT]
    content = content * lax.rsqrt(jnp.mean(jnp.square(content), axis=-1, keepdims=True) + EPS) * kv_gain[...]
    new_latent[:, 0:LAT] = content.astype(BF16)
    new_latent[:, LAT:KVW] = comp[:, LAT:KVW].astype(BF16)

    for i in range(8):
        row = new_latent[i : i + 1, :].astype(F32)
        score = jnp.sum(qv[i].astype(F32) * row, axis=1, keepdims=True) * SCORE_SCALE
        peak_cache = peaks[i][:, 0:1]
        peak = jnp.maximum(peak_cache, score)
        a = jnp.exp(peak_cache - peak)
        b = jnp.exp(score - peak)
        inv = 1.0 / (a * sums[i][:, 0:1] + b)
        context[i] = ((a * inv) * summed[i] + (b * inv) * row[:, 0:LAT]).astype(BF16)

    for copy in sent:
        copy.wait_send()
    latent_step(lambda one, two, three, share: [c.wait_send() for c in one + two + three + [share]])


share_at = 13


def shards(
    hidden_in,
    expert_ids,
    gate_values,
    ffn_gain,
    w_gate,
    w_up,
    w_down,
    attn_gain,
    w_latent,
    kv_gain,
    queries,
    cache,
    lengths,
):
    vmem = pl.BlockSpec(memory_space=pltpu.VMEM)
    smem = pl.BlockSpec(memory_space=pltpu.SMEM)
    hbm = pl.BlockSpec(memory_space=pl.ANY)
    v = pltpu.VMEM
    scatter_bufs = []
    for p in range(3):
        order, w = SCATTER[p], WIDTH[p]
        stages = []
        shape = [4, 4, 4]
        for s in (0, 1):
            shape[DIM[order[s]]] = 1
            half = list(shape)
            half[DIM[order[2]]] = 2
            full, half = (*shape, 16, w), (*half, 16, w)
            stages.append((v(half, BF16), v(half, BF16), v(full, BF16), v(full, BF16), v(full, BF16)))
        stages.append(v((3, 1, 1, 1, 16, w), BF16))
        scatter_bufs.append(tuple(stages))
    scratch = [
        v((D, FFD), BF16),
        v((D, FFD), BF16),
        v((FFD, D), BF16),
        v((4, 4, 112, KVW), BF16),
        v((8, 64, KVW), BF16),
        v((8, 256, KVW), BF16),
        v((8, 64, LAT), F32),
        v((8, 64, 128), F32),
        v((8, 64, 128), F32),
        v((4, 4, SLICE), BF16),
        v((4, 128), F32),
        v((4, 4, SLICE), BF16),
        v((4, 4, 128), F32),
        v((16, SLICE), F32),
        v((4, 4, 4, 16, 640), BF16),
        v((4, 4, 4, 16, 640), BF16),
        v((4, 4, 4, 16, 640), BF16),
        v((256, FFD), F32),
        v((256, FFD), F32),
        v((256, 1), F32),
        v((256, FFD), BF16),
        v((4, 4, 4, 16, WIDTH[0]), BF16),
        v((4, 4, 4, 16, WIDTH[1]), BF16),
        v((4, 4, 4, 16, WIDTH[2]), BF16),
        tuple(scatter_bufs),
        v((16, SLICE), BF16),
        v((4, 4, KVW + 64), F32),
        v((4, 2, 4, KVW + 64), F32),
        pltpu.SemaphoreType.DMA((128,)),
        pltpu.SemaphoreType.DMA((128,)),
        pltpu.SemaphoreType.DMA((16,)),
    ]
    return pl.pallas_call(
        kernel,
        out_shape=(
            jax.ShapeDtypeStruct((8, KVW), BF16),
            jax.ShapeDtypeStruct((8, 64, LAT), BF16),
        ),
        in_specs=[vmem] * 6 + [smem] + [hbm] * 6,
        out_specs=(vmem, vmem),
        scratch_shapes=scratch,
        compiler_params=pltpu.CompilerParams(
            collective_id=0,
            has_side_effects=True,
            vmem_limit_bytes=60 * 1024 * 1024,
        ),
        cost_estimate=pl.CostEstimate(flops=6 * 10**9, bytes_accessed=26 * 10**6, transcendentals=10**6),
    )(
        hidden_in,
        expert_ids,
        gate_values,
        ffn_gain.reshape(1, D),
        attn_gain.reshape(1, D),
        kv_gain.reshape(1, LAT),
        lengths,
        w_gate,
        w_up,
        w_down,
        w_latent,
        queries,
        cache,
    )


def solution(mesh):
    in_specs = (
        P("dev", None),
        P("dev", None),
        P("dev", None),
        P(),
        P(None, "dev"),
        P(None, "dev"),
        P("dev", None),
        P(),
        P("dev", None),
        P(),
        P("dev", None, None),
        P("dev", None, None),
        P("dev"),
    )
    out_specs = (P("dev", None), P("dev", "role", None))
    return jax.shard_map(shards, mesh=mesh, in_specs=in_specs, out_specs=out_specs, check_vma=False)
```

time: 404 us -> 90.1 us (0.22)
  waiting for transfers between devices: 287 us -> 0 us
  Pallas kernels: 0 us -> 80.9 us
  starting transfers between devices: 35.2 us -> 0 us
  matrix products: 28 us -> 0 us
  other arithmetic: 16.4 us -> 0 us
  blocking collectives: 15.5 us -> 0 us
  between operations: 14.9 us -> 0.65 us
    all_to_all x2 -> x0, waiting for transfers between devices: 175 us -> none  [the longest x1 97.5 us: moe_latent(): lax.all_to_all(outgoing, 'dev', split_axis=0, concat_axis=0, tiled=True)]
    unnamed x2 -> x0, waiting for transfers between devices: 112 us -> none
    pallas_call x0 -> x1, Pallas kernels: none -> 80.9 us  [shards(): pl.pallas_call(kernel, out_shape=(jax.ShapeDtypeStruct((8, KVW), BF16), j...]
    dot_general x4 -> x0, matrix products: 28 us -> none  [the longest x1 16.4 us: compute(): jnp.dot(hidden_act, w_down, preferred_element_type=jnp.float32)]
    all_to_all x2 -> x0, starting transfers between devices: 24.7 us -> none  [the longest x1 12.5 us: moe_latent(): lax.all_to_all(produced, 'dev', split_axis=0, concat_axis=0, tiled=True)]
    all_to_all x1 -> x0, blocking collectives: 15.5 us -> none  [moe_latent(): lax.all_to_all(attn_in, 'dev', split_axis=1, concat_axis=0, tiled=True)]
    ppermute x4 -> x0, starting transfers between devices: 10.5 us -> none  [partner_2(): return lax.ppermute(block, axis, route)]
    unnamed x17 -> x6, local copies, waits for them, and re-layouts: 1.29 us -> 8.27 us
  transfers between devices with their start and end apart: 7 -> 0, of which waited for: 3 -> 0; matrix products, arithmetic and copies ran while one was open for 3% -> 0% of each run, Pallas kernels for 0% -> 0%
where the time goes in v1:
time: 90.1 us; the launch traced here: 89.9 us
  Pallas kernels  80.9 us (90%)
  local copies, waits for them, and re-layouts  8.27 us (9%)
    pallas_call x1, Pallas kernels, shards(): pl.pallas_call(kernel, out_shape=(jax.ShapeDtypeStruct((8, KVW), BF16), j...  80.9 us
    unnamed x6, local copies, waits for them, and re-layouts  8.27 us

profile of v1, /device:TPU:1, one launch (start us, length us, event | category | flops | bytes accessed | tf_op | source)
XLA Modules:
  0.0 89.9 jit_solution(10520943032373464019)
XLA Ops:
  0.6 0.0 copy-start
  0.6 2.5 %copy.15.queries = bf16[8,128,576]{2,1,0:T(8,128)(2,1)} copy(bf16[8,128,576]{1,2,0:T(8,128)(2,1)} %param.23) | data formatting | bytes 2359296 | tf_op args[10]
  3.2 0.0 copy-done
  3.2 2.6 %copy.16.cache = bf16[8,256,576]{2,1,0:T(8,128)(2,1)} copy(bf16[8,256,576]{1,2,0:T(8,128)(2,1)S(1)} %copy-done) | data formatting | bytes 4718592 | tf_op args[11]
  5.7 80.9 %shard_map.140 = (bf16[8,576]{1,0:T(8,128)(2,1)}, bf16[8,64,512]{2,1,0:T(8,128)(2,1)}) custom-call(bf16[8,7168]{1,0:T(8,128)(2,1)} %hidden.1, s32[8,8]{1,0:T(8,128)} %ids.1, f32[8,8]{1,0:T(8,128)} %gates.1, f32[1,7168]{1,0:T(1,128)} %bitcast.3, f32[1,7168]{1,0:T(1,128)} %bitcast.4, f32[1,512]{1,0:T(1,128)} %bitcast.5, s32[8]{0:T(128)} %lengths.1, ...), custom_call_target="tpu_custom_call" | custom-call | flops 6000000000 | bytes 26000000 | tf_op jit(solution)/shard_map/pallas_call | solution.py:569
  86.7 1.3 %copy.19 = bf16[8,576]{1,0:T(8,128)(2,1)} copy(bf16[8,576]{1,0:T(8,128)(2,1)} %get-tuple-element.4) | data formatting | bytes 18432
  88.0 1.9 %copy.20 = bf16[8,64,512]{2,1,0:T(8,128)(2,1)} copy(bf16[8,64,512]{2,1,0:T(8,128)(2,1)} %get-tuple-element.5) | data formatting | bytes 1048576
Async XLA Ops:
  0.6 2.6 %copy-start = (bf16[8,256,576]{1,2,0:T(8,128)(2,1)S(1)}, bf16[8,256,576]{1,2,0:T(8,128)(2,1)}, u32[]{:S(2)}) copy-start(bf16[8,256,576]{1,2,0:T(8,128)(2,1)} %param.24) | copy-start | bytes 7077892

commit v2 on v1

--- a/solution.py
+++ b/solution.py
@@ -19,8 +19,10 @@
 EXPERTS = 16
 WIDTH = (640, 640, 512)
 OFF = (0, 640, 1280)
+BASE = (0, 2560, 5120)
 GATHER = (("x", "y", "z"), ("y", "z", "x"), ("z", "x", "y"))
 SCATTER = tuple(order[::-1] for order in GATHER)
+HALVED = ("x", "z", "z")
 DIM = {"z": 0, "x": 1, "y": 2}
 LOW_ROWS = 64
 
@@ -41,10 +43,10 @@
     cache,
     new_latent,
     context,
-    wg,
-    wu,
+    wgu,
     wd,
     wl,
+    qt,
     qv,
     cv,
     summed,
@@ -58,8 +60,7 @@
     ga,
     gb,
     gc,
-    acc_g,
-    acc_u,
+    acc,
     gate_col,
     act,
     oa,
@@ -109,16 +110,12 @@
 
     def load(src, dst):
         copy = pltpu.make_async_copy(src, dst, load_sems.at[len(loads)])
-        copy.start()
+        copy.start(priority=1)
         loads.append(copy)
         return copy
 
-    load_q = load(queries.at[:, pl.ds(pl.multiple_of(role * 64, 64), 64), :], qv)
+    load_q = load(queries, qt)
     load_c = load(cache, cv)
-    load_g = [load(w_gate.at[pl.ds(i * SLICE, SLICE)], wg.at[pl.ds(i * SLICE, SLICE)]) for i in range(4)]
-    load_u = [load(w_up.at[pl.ds(i * SLICE, SLICE)], wu.at[pl.ds(i * SLICE, SLICE)]) for i in range(4)]
-    load_d = [load(w_down.at[pl.ds(i * 128, 128)], wd.at[pl.ds(i * 128, 128)]) for i in range(4)]
-
     barrier = pltpu.get_barrier_semaphore()
     partners = [(role, near(axis, d)) for axis in "xyz" for d in (1, 2, 3)]
     partners += [(1 - role, near("z", d)) for d in (0, 1, 2, 3)]
@@ -143,6 +140,16 @@
     for d in (2, 1, 3):
         first.append(go(remote(xh.at[plus("z", d)], yh.at[z], near("z", d))))
         first.append(go(remote(xe, ye.at[z], near("z", d))))
+
+    load_gu, load_d = [], []
+    pieces = [(p, i) for p in range(3) for i in range(4)]
+    for p, i in pieces:
+        here, there = pl.ds(i * SLICE + OFF[p], WIDTH[p]), pl.ds(BASE[p] + i * WIDTH[p], WIDTH[p])
+        load_gu.append(load(w_gate.at[here], wgu.at[there, pl.ds(0, FFD)]))
+        load_gu.append(load(w_up.at[here], wgu.at[there, pl.ds(FFD, FFD)]))
+    for p, i in pieces:
+        here, there = pl.ds(i * SLICE + OFF[p], WIDTH[p]), pl.ds(BASE[p] + i * WIDTH[p], WIDTH[p])
+        load_d.append(load(w_down.at[:, here], wd.at[:, there]))
 
     def latent_copies():
         out = []
@@ -159,14 +166,14 @@
             ]
 
             def place(pos, half, a=a, rows=rows):
-                full = pl.ds(0, 4) if half is None else pl.ds(2 * half, 2)
+                full = pl.ds(2 * half, 2)
                 return wl.at[pos, full, rows] if a == "x" else wl.at[full, pos, rows]
 
-            two = [remote(place(at[b], None), place(at[b], None), near(b, d)) for d in (1, 3)]
-            three = [
-                remote(place(plus(b, -1), 0), place(plus(b, -1), 0), near(b, 1)),
-                remote(place(plus(b, 1), 1), place(plus(b, 1), 1), near(b, 3)),
-            ]
+            def send(pos, half, d, b=b, place=place):
+                return remote(place(pos, half), place(pos, half), near(b, d))
+
+            two = [send(at[b], 0, 1), send(at[b], 1, 3), send(at[b], 1, 1), send(at[b], 0, 3)]
+            three = [send(plus(b, -1), 0, 1), send(plus(b, 1), 1, 3)]
             share = remote(wl.at[:, :, rows], wl.at[:, :, rows], dev, 1 - role)
             out.append((r, one, two, three, share))
             if r == 0:
@@ -186,7 +193,7 @@
 
         @pl.when(role == r)
         def _(rows=rows):
-            own_rows = pltpu.make_async_copy(w_latent.at[rows], wl.at[y, x, rows], load_sems.at[15])
+            own_rows = pltpu.make_async_copy(w_latent.at[rows], wl.at[y, x, rows], load_sems.at[63])
             own_rows.start()
             own_rows.wait()
 
@@ -226,30 +233,44 @@
     def gather_start(p, k):
         order, ref = GATHER[p], gathered[p]
         a = order[k]
-        here = ref.at[spot(order, k, at[a])]
-        copies = [go(remote(here, here, near(a, d))) for d in ((1, 3) if k else (2, 1, 3))]
-        gstate[p] = copies
+        if k < 2:
+            here = ref.at[spot(order, k, at[a])]
+            gstate[p] = [go(remote(here, here, near(a, d))) for d in (2, 1, 3)]
+            return
+        gstate[p] = []
+        for half, d in ((0, 1), (1, 3)):
+            here = ref.at[spot(order, k, at[a], half)]
+            gstate[p].append(go(remote(here, here, near(a, d))))
+
+    def gather_rest(p, k):
+        order, ref = GATHER[p], gathered[p]
+        a = order[k]
+        for half, d in ((1, 1), (0, 3)):
+            here = ref.at[spot(order, k, at[a], half)]
+            gstate[p].append(go(remote(here, here, near(a, d))))
 
     def gather_forward(p, k):
         order, ref = GATHER[p], gathered[p]
         a = order[k]
-        right, left = gstate[p]
-        right.wait_recv()
+        gstate[p][0].wait_recv()
         one = ref.at[spot(order, k, plus(a, -1), 0)]
         one = go(remote(one, one, near(a, 1)))
-        left.wait_recv()
+        gstate[p][1].wait_recv()
         two = ref.at[spot(order, k, plus(a, 1), 1)]
         two = go(remote(two, two, near(a, 3)))
-        gstate[p] = [one, two]
-
-    def gather_finish(p):
-        for copy in gstate[p]:
+        gstate[p] = gstate[p][2:] + [one, two]
+
+    def gather_wait(p, n):
+        for copy in gstate[p][:n]:
             copy.wait_recv()
+        gstate[p] = gstate[p][n:]
 
     def attend(lo, hi):
         @pl.loop(lo, hi)
         def _(i):
-            s = lax.dot_general(qv[i], cv[i], (((1,), (1,)), ((), ())), preferred_element_type=F32)
+            both = qt[i].T
+            qv[i] = jnp.where(role == 0, both[0:64], both[64:128])
+            s = jnp.dot(qv[i], cv[i], preferred_element_type=F32)
             s = s * SCORE_SCALE
             live = lax.broadcasted_iota(jnp.int32, (64, 256), 1) < lengths[i]
             s = jnp.where(live, s, -jnp.inf)
@@ -257,64 +278,62 @@
             w = jnp.where(live, jnp.exp(s - peak), 0.0).astype(BF16)
             sums[i] = jnp.broadcast_to(jnp.sum(w.astype(F32), axis=1, keepdims=True), (64, 128))
             peaks[i] = jnp.broadcast_to(peak, (64, 128))
-            summed[i] = jnp.dot(w, cv[i, :, 0:LAT], preferred_element_type=F32)
-
-    def gate_up(p, zz):
-        rows = gathered[p][zz].reshape(256, 640)
-        if p == 2:
-            rows = rows[:, 0:512]
-        k = pl.ds(pl.multiple_of(zz * SLICE + OFF[p], 128), WIDTH[p])
-        acc_g[...] += jnp.dot(rows, wg[k, :], preferred_element_type=F32)
-        acc_u[...] += jnp.dot(rows, wu[k, :], preferred_element_type=F32)
+            summed[i] = lax.dot_general(
+                w, cv[i, 0:LAT, :], (((1,), (1,)), ((), ())), preferred_element_type=F32
+            )
+
+    def gate_up_slice(zz, first=False):
+        k = pl.ds(pl.multiple_of(BASE[0] + zz * WIDTH[0], 128), WIDTH[0])
+
+        @pl.loop(0, 2)
+        def _(n):
+            cols = pl.ds(pl.multiple_of(n * 512, 512), 512)
+            rows = ga[zz].reshape(256, WIDTH[0])
+            out = jnp.dot(rows, wgu[k, cols], preferred_element_type=F32).reshape(4, 4, 16, 512)
+            acc[..., cols] = out if first else acc[..., cols] + out
+
+    def gate_up_rows(*ds):
+        for p in (1, 2):
+            picks = []
+            for d in ds:
+                axis = GATHER[p][2]
+                picks.append((plus("x", d), slice(None)) if axis == "x" else (slice(None), plus("y", d)))
+
+            @pl.loop(0, 1)
+            def _(n, p=p, picks=picks):
+                cols = pl.ds(pl.multiple_of(n * 1024, 1024), 1024)
+                rows = [
+                    jnp.concatenate(
+                        [gathered[p][i, a, b, :, 0 : WIDTH[p]].reshape(64, WIDTH[p]) for i in range(4)], axis=1
+                    )
+                    for a, b in picks
+                ]
+                rows = jnp.concatenate(rows, axis=0) if len(rows) > 1 else rows[0]
+                out = jnp.dot(rows, wgu[pl.ds(BASE[p], 4 * WIDTH[p]), cols], preferred_element_type=F32)
+                for i, (a, b) in enumerate(picks):
+                    acc[a, b, :, cols] += out[64 * i : 64 * i + 64].reshape(4, 16, 1024)
 
     for p in range(3):
         gather_start(p, 0)
     load_q.wait()
     load_c.wait()
-    for p in range(3):
-        gather_finish(p)
+    attend(0, 4)
+    for p in range(3):
+        gather_wait(p, 3)
         gather_start(p, 1)
-    attend(0, 4)
-    for p in range(3):
-        gather_forward(p, 1)
+    latent_step(lambda one, two, three, share: [c.wait_recv() for c in one] + [c.start() for c in two])
     attend(4, 8)
     for p in range(3):
-        gather_finish(p)
+        gather_wait(p, 3)
         gather_start(p, 2)
-    latent_step(lambda one, two, three, share: [c.wait_recv() for c in one])
-    for copy in load_g + load_u:
+    for p in range(3):
+        gather_rest(p, 2)
+    for copy in load_gu:
         copy.wait()
-    acc_g[...] = jnp.zeros_like(acc_g)
-    acc_u[...] = jnp.zeros_like(acc_u)
-    gate_up(0, z)
+    gate_up_slice(z, True)
+    gate_up_rows(0)
     for p in range(3):
         gather_forward(p, 2)
-    latent_step(lambda one, two, three, share: [c.start() for c in two])
-    gate_up(0, plus("z", 1))
-    gate_up(0, plus("z", 3))
-    for p in range(3):
-        gather_finish(p)
-    gate_up(0, plus("z", 2))
-    for p in (1, 2):
-
-        @pl.loop(0, 4)
-        def _(zz, p=p):
-            gate_up(p, zz)
-
-    expert = z * 4 + y
-    mine = lax.broadcasted_iota(jnp.int32, (256, 128), 1)
-    mine = jnp.logical_or(mine == expert, mine == expert + EXPERTS)
-    table_all = gc[0, :, :, :, 512:640].reshape(256, 128).astype(F32)
-    gate_col[...] = jnp.sum(jnp.where(mine, table_all, 0.0), axis=1, keepdims=True)
-
-    @pl.loop(0, 16)
-    def _(i):
-        rows = pl.ds(pl.multiple_of(i * 16, 16), 16)
-        g = acc_g[rows, :]
-        act[rows, :] = (g / (1.0 + jnp.exp(-g)) * acc_u[rows, :] * gate_col[rows, :]).astype(BF16)
-
-    for copy in load_d:
-        copy.wait()
     latent_step(
         lambda one, two, three, share: [
             two[0].wait_recv(),
@@ -323,13 +342,41 @@
             three[1].start(),
         ]
     )
+    for p in range(3):
+        gather_wait(p, 2)
+    gate_up_slice(plus("z", 1))
+    gate_up_slice(plus("z", 3))
+    gate_up_rows(1, 3)
+    gather_wait(0, 2)
+    gate_up_slice(plus("z", 2))
+    gather_wait(1, 2)
+    gather_wait(2, 2)
+    gate_up_rows(2)
+
+    expert = z * 4 + y
+    mine = lax.broadcasted_iota(jnp.int32, (256, 128), 1)
+    mine = jnp.logical_or(mine == expert, mine == expert + EXPERTS)
+    table_all = gc[0, :, :, :, 512:640].reshape(256, 128).astype(F32)
+    gate_col[...] = jnp.sum(jnp.where(mine, table_all, 0.0), axis=1, keepdims=True)
+
+    @pl.loop(0, 8)
+    def _(i):
+        rows = pl.ds(pl.multiple_of(i * 32, 32), 32)
+        half = pl.ds(pl.multiple_of(lax.rem(i, 2) * 2, 2), 2)
+        g = acc[i // 2, half, :, 0:FFD].reshape(32, FFD)
+        u = acc[i // 2, half, :, FFD:].reshape(32, FFD)
+        act[rows, :] = (g / (1.0 + jnp.exp(-g)) * u * gate_col[rows, :]).astype(BF16)
+
+    for copy in load_d:
+        copy.wait()
 
     outs = (oa, ob, oc)
 
-    def down(p, zz):
-        k = pl.ds(pl.multiple_of(zz * SLICE + OFF[p], 128), WIDTH[p])
-        out = jnp.dot(act[...], wd[:, k], preferred_element_type=F32)
-        outs[p][zz] = out.astype(BF16).reshape(4, 4, 16, WIDTH[p])
+    def down(p, zz, n=1):
+        k = pl.ds(pl.multiple_of(BASE[p] + zz * WIDTH[p], 128), n * WIDTH[p])
+        out = jnp.dot(act[...], wd[:, k], preferred_element_type=F32).astype(BF16)
+        for i in range(n):
+            outs[p][zz + i] = out[:, i * WIDTH[p] : (i + 1) * WIDTH[p]].reshape(4, 4, 16, WIDTH[p])
 
     def block(order, s, value, half=None):
         spec = {}
@@ -339,23 +386,22 @@
         for axis in order[s + 1 :]:
             spec[axis] = pl.ds(0, 4)
         if half is not None:
-            spec[order[2]] = pl.ds(2 * half, 2)
+            spec[HALVED[SCATTER.index(order)]] = pl.ds(2 * half, 2)
         return spec["z"], spec["x"], spec["y"]
 
     def part_of(order, half):
         spec = {axis: slice(None) for axis in order}
-        spec[order[2]] = pl.ds(2 * half, 2)
+        spec[HALVED[SCATTER.index(order)]] = pl.ds(2 * half, 2)
         return spec["z"], spec["x"], spec["y"]
 
-    sstate = [None] * 3
-
-    def scatter_opposite(p, s, cur):
+    sstate = [[], [], []]
+
+    def scatter_opposite(p, s, cur, half):
         order = SCATTER[p]
         b = order[s]
-        fl, fr, rl, rr, out = rs_bufs[p][s]
-        one = go(remote(cur.at[block(order, s, plus(b, 2), 0)], fl, near(b, 1)))
-        two = go(remote(cur.at[block(order, s, plus(b, 2), 1)], fr, near(b, 3)))
-        sstate[p] = [one, two]
+        to = rs_bufs[p][s][half]
+        d = (1, 3)[half]
+        sstate[p].append(go(remote(cur.at[block(order, s, plus(b, 2), half)], to, near(b, d))))
 
     def scatter_direct(p, s, cur):
         order = SCATTER[p]
@@ -394,39 +440,40 @@
         return out
 
     down(0, plus("z", 2))
-    scatter_opposite(0, 0, oa)
+    scatter_opposite(0, 0, oa, 0)
+    scatter_opposite(0, 0, oa, 1)
+    for p in (1, 2):
+        for half in (0, 1):
+            down(p, 2 * half, 2)
+            scatter_opposite(p, 0, outs[p], half)
+        scatter_direct(p, 0, outs[p])
     down(0, plus("z", 1))
     down(0, plus("z", 3))
     scatter_direct(0, 0, oa)
-    for p in (1, 2):
-
-        @pl.loop(0, 4)
-        def _(zz, p=p):
-            down(p, zz)
-
-        scatter_opposite(p, 0, outs[p])
-        scatter_direct(p, 0, outs[p])
     down(0, z)
     cur = list(outs)
     for p in range(3):
         scatter_forward(p, 0, cur[p])
-    latent_step(lambda one, two, three, share: [three[0].wait_recv(), three[1].wait_recv(), share.start()])
-    for s in (0, 1):
-        for p in range(3):
-            cur[p] = scatter_finish(p, s, cur[p])
-            if s == 0:
-                scatter_opposite(p, 1, cur[p])
-                scatter_direct(p, 1, cur[p])
-            else:
-                order = SCATTER[p]
-                b = order[2]
-                slots = rs_bufs[p][2]
-                sstate[p] = [
-                    go(remote(cur[p].at[block(order, 2, plus(b, d))], slots.at[d - 1], near(b, d))) for d in (2, 1, 3)
-                ]
-        if s == 0:
-            for p in range(3):
-                scatter_forward(p, 1, cur[p])
+    latent_step(lambda one, two, three, share: [c.wait_recv() for c in two[2:] + three] + [share.start()])
+    def scatter_all(p, s):
+        order = SCATTER[p]
+        b = order[s]
+        slots = rs_bufs[p][s][0]
+        sstate[p] = [
+            go(remote(cur[p].at[block(order, s, plus(b, d))], slots.at[d - 1], near(b, d))) for d in (2, 1, 3)
+        ]
+
+    for p in range(3):
+        cur[p] = scatter_finish(p, 0, cur[p])
+        scatter_all(p, 1)
+    for p in range(3):
+        order = SCATTER[p]
+        slots, out = rs_bufs[p][1]
+        for copy in sstate[p]:
+            copy.wait_recv()
+        add_into(out, [cur[p][block(order, 1, at[order[1]])]] + [slots[d] for d in range(3)])
+        cur[p] = out
+        scatter_all(p, 2)
 
     squares = jnp.zeros((16, 1), F32)
     for p in range(3):
@@ -435,7 +482,7 @@
             copy.wait_recv()
         total = cur[p][block(order, 2, at[order[2]])].reshape(16, WIDTH[p]).astype(F32)
         for d in range(3):
-            total = total + rs_bufs[p][2][d].reshape(16, WIDTH[p]).astype(F32)
+            total = total + rs_bufs[p][2][0][d].reshape(16, WIDTH[p]).astype(F32)
         cols = slice(OFF[p], OFF[p] + WIDTH[p])
         residual = (hid16[:, cols] + total).astype(BF16).astype(F32)
         squares = squares + jnp.sum(jnp.square(residual), axis=1, keepdims=True)
@@ -498,7 +545,7 @@
     latent_step(lambda one, two, three, share: [c.wait_send() for c in one + two + three + [share]])
 
 
-share_at = 13
+share_at = 15
 
 
 def shards(
@@ -525,21 +572,25 @@
         order, w = SCATTER[p], WIDTH[p]
         stages = []
         shape = [4, 4, 4]
-        for s in (0, 1):
+        for s in range(3):
             shape[DIM[order[s]]] = 1
-            half = list(shape)
-            half[DIM[order[2]]] = 2
-            full, half = (*shape, 16, w), (*half, 16, w)
-            stages.append((v(half, BF16), v(half, BF16), v(full, BF16), v(full, BF16), v(full, BF16)))
-        stages.append(v((3, 1, 1, 1, 16, w), BF16))
+            full = (*shape, 16, w)
+            half = list(full)
+            half[DIM[HALVED[p]]] = 2
+            if s == 0:
+                stages.append((v(half, BF16), v(half, BF16), v(full, BF16), v(full, BF16), v(full, BF16)))
+            elif s == 1:
+                stages.append((v((3, *full), BF16), v(full, BF16)))
+            else:
+                stages.append((v((3, *full), BF16),))
         scatter_bufs.append(tuple(stages))
     scratch = [
-        v((D, FFD), BF16),
-        v((D, FFD), BF16),
+        v((D, 2 * FFD), BF16),
         v((FFD, D), BF16),
         v((4, 4, 112, KVW), BF16),
+        v((8, KVW, 128), BF16),
         v((8, 64, KVW), BF16),
-        v((8, 256, KVW), BF16),
+        v((8, KVW, 256), BF16),
         v((8, 64, LAT), F32),
         v((8, 64, 128), F32),
         v((8, 64, 128), F32),
@@ -551,8 +602,7 @@
         v((4, 4, 4, 16, 640), BF16),
         v((4, 4, 4, 16, 640), BF16),
         v((4, 4, 4, 16, 640), BF16),
-        v((256, FFD), F32),
-        v((256, FFD), F32),
+        v((4, 4, 16, 2 * FFD), F32),
         v((256, 1), F32),
         v((256, FFD), BF16),
         v((4, 4, 4, 16, WIDTH[0]), BF16),
@@ -564,7 +614,7 @@
         v((4, 2, 4, KVW + 64), F32),
         pltpu.SemaphoreType.DMA((128,)),
         pltpu.SemaphoreType.DMA((128,)),
-        pltpu.SemaphoreType.DMA((16,)),
+        pltpu.SemaphoreType.DMA((64,)),
     ]
     return pl.pallas_call(
         kernel,
@@ -593,8 +643,8 @@
         w_up,
         w_down,
         w_latent,
-        queries,
-        cache,
+        jnp.transpose(queries, (0, 2, 1)),
+        jnp.transpose(cache, (0, 2, 1)),
     )
 
 

time: 90.1 us -> 73.8 us (0.82)
  Pallas kernels: 80.9 us -> 69.7 us
  local copies, waits for them, and re-layouts: 8.27 us -> 3.17 us
    pallas_call x1, Pallas kernels: 80.9 us -> 69.7 us  [shards(): pl.pallas_call(kernel, out_shape=(jax.ShapeDtypeStruct((8, KVW), BF16), j...]
    unnamed x6 -> x2, local copies, waits for them, and re-layouts: 8.27 us -> 3.17 us
where the time goes in v2:
time: 73.8 us; the launch traced here: 73.5 us
  Pallas kernels  69.7 us (94%)
  local copies, waits for them, and re-layouts  3.17 us (4%)
    pallas_call x1, Pallas kernels, shards(): pl.pallas_call(kernel, out_shape=(jax.ShapeDtypeStruct((8, KVW), BF16), j...  69.7 us
    unnamed x2, local copies, waits for them, and re-layouts  3.17 us

profile of v2, /device:TPU:1, one launch (start us, length us, event | category | flops | bytes accessed | tf_op | source)
XLA Modules:
  0.0 73.5 jit_solution(18206358606849216514)
XLA Ops:
  0.6 69.7 %shard_map.140 = (bf16[8,576]{1,0:T(8,128)(2,1)}, bf16[8,64,512]{2,1,0:T(8,128)(2,1)}) custom-call(bf16[8,7168]{1,0:T(8,128)(2,1)} %hidden.1, s32[8,8]{1,0:T(8,128)} %ids.1, f32[8,8]{1,0:T(8,128)} %gates.1, f32[1,7168]{1,0:T(1,128)} %bitcast.7, f32[1,7168]{1,0:T(1,128)} %bitcast.8, f32[1,512]{1,0:T(1,128)} %bitcast.9, s32[8]{0:T(128)} %lengths.1, ...), custom_call_target="tpu_custom_call" | custom-call | flops 6000000000 | bytes 26000000 | tf_op jit(solution)/shard_map/pallas_call | solution.py:619
  70.4 1.3 %copy.17 = bf16[8,576]{1,0:T(8,128)(2,1)} copy(bf16[8,576]{1,0:T(8,128)(2,1)} %get-tuple-element.4) | data formatting | bytes 18432
  71.7 1.9 %copy.18 = bf16[8,64,512]{2,1,0:T(8,128)(2,1)} copy(bf16[8,64,512]{2,1,0:T(8,128)(2,1)} %get-tuple-element.5) | data formatting | bytes 1048576

commit v3 on v2

--- a/solution.py
+++ b/solution.py
@@ -24,16 +24,19 @@
 SCATTER = tuple(order[::-1] for order in GATHER)
 HALVED = ("x", "z", "z")
 DIM = {"z": 0, "x": 1, "y": 2}
+SEND_RING = 44
+COPIES = 95
+LOADS = 46
 LOW_ROWS = 64
 
 
 def kernel(
-    hidden,
-    ids,
-    gates,
-    ffn_gain,
-    attn_gain,
-    kv_gain,
+    hidden_in,
+    ids_in,
+    gates_in,
+    ffn_gain_in,
+    attn_gain_in,
+    kv_gain_in,
     lengths,
     w_gate,
     w_up,
@@ -42,7 +45,14 @@
     queries,
     cache,
     new_latent,
-    context,
+    factors,
+    summed_out,
+    hidden,
+    ids,
+    gates,
+    ffn_gain,
+    attn_gain,
+    kv_gain,
     wgu,
     wd,
     wl,
@@ -67,7 +77,6 @@
     ob,
     oc,
     rs_bufs,
-    att,
     tbuf,
     ebuf,
     send_sems,
@@ -89,13 +98,17 @@
     count = [0]
     sent = []
 
-    def remote(src, dst, to_dev, to_role=None):
+    def remote(src, dst, to_dev, to_role=None, send_at=None):
         i = count[0]
         count[0] += 1
+        if send_at is None:
+            if len(sent) >= SEND_RING:
+                sent[-SEND_RING].wait_send()
+            send_at = len(sent) % SEND_RING
         return pltpu.make_async_remote_copy(
             src_ref=src,
             dst_ref=dst,
-            send_sem=send_sems.at[i],
+            send_sem=send_sems.at[send_at],
             recv_sem=recv_sems.at[i],
             device_id=(role if to_role is None else to_role, to_dev),
             device_id_type=MESH,
@@ -114,14 +127,25 @@
         loads.append(copy)
         return copy
 
-    load_q = load(queries, qt)
-    load_c = load(cache, cv)
     barrier = pltpu.get_barrier_semaphore()
     partners = [(role, near(axis, d)) for axis in "xyz" for d in (1, 2, 3)]
     partners += [(1 - role, near("z", d)) for d in (0, 1, 2, 3)]
     for partner in partners:
         pl.semaphore_signal(barrier, inc=1, device_id=partner, device_id_type=MESH)
 
+    small = (
+        load(hidden_in, hidden),
+        load(ids_in, ids),
+        load(gates_in, gates),
+        load(ffn_gain_in, ffn_gain),
+        load(attn_gain_in, attn_gain),
+        load(kv_gain_in, kv_gain),
+    )
+    load_q = load(queries, qt)
+    load_c = load(cache, cv)
+
+    for copy in small:
+        copy.wait()
     hid = hidden[...].astype(F32)
     scale = lax.rsqrt(jnp.mean(jnp.square(hid), axis=-1, keepdims=True) + EPS)
     lane = lax.broadcasted_iota(jnp.int32, (8, 128), 1)
@@ -161,6 +185,7 @@
                     wl.at[y, x, rows],
                     wl.at[y, x, rows],
                     near(a, d),
+                    send_at=SEND_RING + d - 1,
                 )
                 for d in (2, 1, 3)
             ]
@@ -169,12 +194,12 @@
                 full = pl.ds(2 * half, 2)
                 return wl.at[pos, full, rows] if a == "x" else wl.at[full, pos, rows]
 
-            def send(pos, half, d, b=b, place=place):
-                return remote(place(pos, half), place(pos, half), near(b, d))
-
-            two = [send(at[b], 0, 1), send(at[b], 1, 3), send(at[b], 1, 1), send(at[b], 0, 3)]
-            three = [send(plus(b, -1), 0, 1), send(plus(b, 1), 1, 3)]
-            share = remote(wl.at[:, :, rows], wl.at[:, :, rows], dev, 1 - role)
+            def send(pos, half, d, k, b=b, place=place):
+                return remote(place(pos, half), place(pos, half), near(b, d), send_at=SEND_RING + k)
+
+            two = [send(at[b], 0, 1, 3), send(at[b], 1, 3, 4), send(at[b], 1, 1, 5), send(at[b], 0, 3, 6)]
+            three = [send(plus(b, -1), 0, 1, 7), send(plus(b, 1), 1, 3, 8)]
+            share = remote(wl.at[:, :, rows], wl.at[:, :, rows], dev, 1 - role, SEND_RING + 9)
             out.append((r, one, two, three, share))
             if r == 0:
                 count[0] = base
@@ -193,7 +218,7 @@
 
         @pl.when(role == r)
         def _(rows=rows):
-            own_rows = pltpu.make_async_copy(w_latent.at[rows], wl.at[y, x, rows], load_sems.at[63])
+            own_rows = pltpu.make_async_copy(w_latent.at[rows], wl.at[y, x, rows], load_sems.at[LOADS - 1])
             own_rows.start()
             own_rows.wait()
 
@@ -321,8 +346,8 @@
     for p in range(3):
         gather_wait(p, 3)
         gather_start(p, 1)
-    latent_step(lambda one, two, three, share: [c.wait_recv() for c in one] + [c.start() for c in two])
     attend(4, 8)
+    store_summed = load(summed, summed_out)
     for p in range(3):
         gather_wait(p, 3)
         gather_start(p, 2)
@@ -334,14 +359,7 @@
     gate_up_rows(0)
     for p in range(3):
         gather_forward(p, 2)
-    latent_step(
-        lambda one, two, three, share: [
-            two[0].wait_recv(),
-            three[0].start(),
-            two[1].wait_recv(),
-            three[1].start(),
-        ]
-    )
+    latent_step(lambda one, two, three, share: [c.wait_recv() for c in one] + [c.start() for c in two])
     for p in range(3):
         gather_wait(p, 2)
     gate_up_slice(plus("z", 1))
@@ -454,7 +472,6 @@
     cur = list(outs)
     for p in range(3):
         scatter_forward(p, 0, cur[p])
-    latent_step(lambda one, two, three, share: [c.wait_recv() for c in two[2:] + three] + [share.start()])
     def scatter_all(p, s):
         order = SCATTER[p]
         b = order[s]
@@ -466,6 +483,14 @@
     for p in range(3):
         cur[p] = scatter_finish(p, 0, cur[p])
         scatter_all(p, 1)
+    latent_step(
+        lambda one, two, three, share: [
+            two[0].wait_recv(),
+            three[0].start(),
+            two[1].wait_recv(),
+            three[1].start(),
+        ]
+    )
     for p in range(3):
         order = SCATTER[p]
         slots, out = rs_bufs[p][1]
@@ -474,8 +499,24 @@
         add_into(out, [cur[p][block(order, 1, at[order[1]])]] + [slots[d] for d in range(3)])
         cur[p] = out
         scatter_all(p, 2)
+    latent_step(lambda one, two, three, share: [c.wait_recv() for c in two[2:] + three] + [share.start()])
+
+    for r, one, two, three, share in latent_plan:
+
+        @pl.when(role == r)
+        def _(r=r):
+            rows = pl.ds(LOW_ROWS, 112 - LOW_ROWS) if r == 0 else pl.ds(0, LOW_ROWS)
+            pltpu.make_async_remote_copy(
+                src_ref=wl.at[:, :, rows],
+                dst_ref=wl.at[:, :, rows],
+                send_sem=send_sems.at[SEND_RING + 9],
+                recv_sem=recv_sems.at[share_at],
+                device_id=(1 - role, dev),
+                device_id_type=MESH,
+            ).wait_recv()
 
     squares = jnp.zeros((16, 1), F32)
+    partial = jnp.zeros((16, KVW), F32)
     for p in range(3):
         order = SCATTER[p]
         for copy in sstate[p]:
@@ -487,22 +528,8 @@
         residual = (hid16[:, cols] + total).astype(BF16).astype(F32)
         squares = squares + jnp.sum(jnp.square(residual), axis=1, keepdims=True)
         gain = attn_gain[:, pl.ds(pl.multiple_of(z * SLICE + OFF[p], 128), WIDTH[p])]
-        att[:, cols] = (residual * gain).astype(BF16)
-    for r, one, two, three, share in latent_plan:
-
-        @pl.when(role == r)
-        def _(r=r):
-            rows = pl.ds(LOW_ROWS, 112 - LOW_ROWS) if r == 0 else pl.ds(0, LOW_ROWS)
-            pltpu.make_async_remote_copy(
-                src_ref=wl.at[:, :, rows],
-                dst_ref=wl.at[:, :, rows],
-                send_sem=send_sems.at[share_at],
-                recv_sem=recv_sems.at[share_at],
-                device_id=(1 - role, dev),
-                device_id_type=MESH,
-            ).wait_recv()
-
-    partial = jnp.dot(att[...], wl[...].reshape(SLICE, KVW), preferred_element_type=F32)
+        w = wl[...].reshape(SLICE, KVW)[cols]
+        partial = partial + jnp.dot((residual * gain).astype(BF16), w, preferred_element_type=F32)
     partial = jnp.concatenate([partial, jnp.broadcast_to(squares, (16, 64))], axis=1)
     for i in range(4):
         tbuf[i] = partial[4 * i : 4 * i + 4]
@@ -530,6 +557,7 @@
     new_latent[:, 0:LAT] = content.astype(BF16)
     new_latent[:, LAT:KVW] = comp[:, LAT:KVW].astype(BF16)
 
+    second = lax.broadcasted_iota(jnp.int32, (64, 128), 1) >= 64
     for i in range(8):
         row = new_latent[i : i + 1, :].astype(F32)
         score = jnp.sum(qv[i].astype(F32) * row, axis=1, keepdims=True) * SCORE_SCALE
@@ -538,14 +566,25 @@
         a = jnp.exp(peak_cache - peak)
         b = jnp.exp(score - peak)
         inv = 1.0 / (a * sums[i][:, 0:1] + b)
-        context[i] = ((a * inv) * summed[i] + (b * inv) * row[:, 0:LAT]).astype(BF16)
-
-    for copy in sent:
+        factors[i] = jnp.where(second, b * inv, a * inv)
+
+    store_summed.wait()
+    assert (count[0], len(loads)) == (COPIES, LOADS - 1), (count[0], len(loads))
+    for copy in sent[-SEND_RING:]:
         copy.wait_send()
     latent_step(lambda one, two, three, share: [c.wait_send() for c in one + two + three + [share]])
 
 
 share_at = 15
+
+
+def merge(new_latent, factors, summed, latent_out, context):
+    latent_out[...] = new_latent[...]
+    rows = new_latent[:, 0:LAT].astype(F32)
+    rows = jnp.where(pl.program_id(0) == 0, rows[0:4], rows[4:8])
+    for i in range(4):
+        row = rows[i : i + 1]
+        context[i] = (factors[i, :, 0:1] * summed[i] + factors[i, :, 64:65] * row).astype(BF16)
 
 
 def shards(
@@ -585,6 +624,12 @@
                 stages.append((v((3, *full), BF16),))
         scatter_bufs.append(tuple(stages))
     scratch = [
+        v((8, D), BF16),
+        v((8, 8), jnp.int32),
+        v((8, 8), F32),
+        v((1, D), F32),
+        v((1, D), F32),
+        v((1, LAT), F32),
         v((D, 2 * FFD), BF16),
         v((FFD, D), BF16),
         v((4, 4, 112, KVW), BF16),
@@ -609,21 +654,21 @@
         v((4, 4, 4, 16, WIDTH[1]), BF16),
         v((4, 4, 4, 16, WIDTH[2]), BF16),
         tuple(scatter_bufs),
-        v((16, SLICE), BF16),
         v((4, 4, KVW + 64), F32),
         v((4, 2, 4, KVW + 64), F32),
-        pltpu.SemaphoreType.DMA((128,)),
-        pltpu.SemaphoreType.DMA((128,)),
-        pltpu.SemaphoreType.DMA((64,)),
+        pltpu.SemaphoreType.DMA((SEND_RING + 10,)),
+        pltpu.SemaphoreType.DMA((COPIES,)),
+        pltpu.SemaphoreType.DMA((LOADS,)),
     ]
-    return pl.pallas_call(
+    state = pl.pallas_call(
         kernel,
         out_shape=(
             jax.ShapeDtypeStruct((8, KVW), BF16),
-            jax.ShapeDtypeStruct((8, 64, LAT), BF16),
+            jax.ShapeDtypeStruct((8, 64, 128), F32),
+            jax.ShapeDtypeStruct((8, 64, LAT), F32),
         ),
-        in_specs=[vmem] * 6 + [smem] + [hbm] * 6,
-        out_specs=(vmem, vmem),
+        in_specs=[hbm] * 6 + [smem] + [hbm] * 6,
+        out_specs=(vmem, vmem, hbm),
         scratch_shapes=scratch,
         compiler_params=pltpu.CompilerParams(
             collective_id=0,
@@ -646,6 +691,23 @@
         jnp.transpose(queries, (0, 2, 1)),
         jnp.transpose(cache, (0, 2, 1)),
     )
+    return pl.pallas_call(
+        merge,
+        grid=(2,),
+        out_shape=(
+            jax.ShapeDtypeStruct((8, KVW), BF16),
+            jax.ShapeDtypeStruct((8, 64, LAT), BF16),
+        ),
+        in_specs=[
+            pl.BlockSpec((8, KVW), lambda i: (0, 0)),
+            pl.BlockSpec((4, 64, 128), lambda i: (i, 0, 0)),
+            pl.BlockSpec((4, 64, LAT), lambda i: (i, 0, 0)),
+        ],
+        out_specs=(
+            pl.BlockSpec((8, KVW), lambda i: (0, 0)),
+            pl.BlockSpec((4, 64, LAT), lambda i: (i, 0, 0)),
+        ),
+    )(*state)
 
 
 def solution(mesh):

time: 73.8 us -> 69.8 us (0.946)
  local copies, waits for them, and re-layouts: 3.17 us -> 0 us
    unnamed x2 -> x0, local copies, waits for them, and re-layouts: 3.17 us -> none
    pallas_call x1, Pallas kernels: 69.7 us -> 66.8 us  [shards(): pl.pallas_call(kernel, out_shape=(jax.ShapeDtypeStruct((8, KVW), BF16), j...]
    pallas_call x0 -> x1, Pallas kernels: none -> 2.2 us  [shards(): pl.pallas_call(merge, grid=(2,), out_shape=(jax.ShapeDtypeStruct((8, KVW)...]
where the time goes in v3:
time: 69.8 us; the launch traced here: 69.7 us
  Pallas kernels  69 us (99%)
    pallas_call x1, Pallas kernels, shards(): pl.pallas_call(kernel, out_shape=(jax.ShapeDtypeStruct((8, KVW), BF16), j...  66.8 us
    pallas_call x1, Pallas kernels, shards(): pl.pallas_call(merge, grid=(2,), out_shape=(jax.ShapeDtypeStruct((8, KVW)...  2.2 us

profile of v3, /device:TPU:1, one launch (start us, length us, event | category | flops | bytes accessed | tf_op | source)
XLA Modules:
  0.0 69.7 jit_solution(4612609816923596500)
XLA Ops:
  0.6 66.8 %shard_map.140 = (bf16[8,576]{1,0:T(8,128)(2,1)}, f32[8,64,128]{2,1,0:T(8,128)}, f32[8,64,512]{2,1,0:T(8,128)}) custom-call(bf16[8,7168]{1,0:T(8,128)(2,1)} %hidden_in.1, s32[8,8]{1,0:T(8,128)} %ids_in.1, f32[8,8]{1,0:T(8,128)} %gates_in.1, f32[1,7168]{1,0:T(1,128)} %bitcast.7, f32[1,7168]{1,0:T(1,128)} %bitcast.8, f32[1,512]{1,0:T(1,128)} %bitcast.9, ...), custom_call_target="tpu_custom_call" | custom-call | flops 6000000000 | bytes 26000000 | tf_op jit(solution)/shard_map/pallas_call | solution.py:663
  67.4 2.2 %shard_map.141 = (bf16[8,576]{1,0:T(8,128)(2,1)}, bf16[8,64,512]{2,1,0:T(8,128)(2,1)}) custom-call(bf16[8,576]{1,0:T(8,128)(2,1)} %get-tuple-element.5.new_latent, f32[8,64,128]{2,1,0:T(8,128)} %get-tuple-element.6.factors, f32[8,64,512]{2,1,0:T(8,128)} %get-tuple-element.7.summed), custom_call_target="tpu_custom_call" | custom-call | tf_op jit(solution)/shard_map/pallas_call | solution.py:694

commit v4 on v3

--- a/solution.py
+++ b/solution.py
@@ -25,7 +25,7 @@
 HALVED = ("x", "z", "z")
 DIM = {"z": 0, "x": 1, "y": 2}
 SEND_RING = 44
-COPIES = 95
+COPIES = 101
 LOADS = 46
 LOW_ROWS = 64
 
@@ -70,6 +70,7 @@
     ga,
     gb,
     gc,
+    gx,
     acc,
     gate_col,
     act,
@@ -171,10 +172,6 @@
         here, there = pl.ds(i * SLICE + OFF[p], WIDTH[p]), pl.ds(BASE[p] + i * WIDTH[p], WIDTH[p])
         load_gu.append(load(w_gate.at[here], wgu.at[there, pl.ds(0, FFD)]))
         load_gu.append(load(w_up.at[here], wgu.at[there, pl.ds(FFD, FFD)]))
-    for p, i in pieces:
-        here, there = pl.ds(i * SLICE + OFF[p], WIDTH[p]), pl.ds(BASE[p] + i * WIDTH[p], WIDTH[p])
-        load_d.append(load(w_down.at[:, here], wd.at[:, there]))
-
     def latent_copies():
         out = []
         for r, rows, axes in ((0, pl.ds(0, LOW_ROWS), "xy"), (1, pl.ds(LOW_ROWS, 112 - LOW_ROWS), "yx")):
@@ -235,10 +232,10 @@
     normed = (h16 * e16[:, 2 * EXPERTS : 2 * EXPERTS + 1] * ffn_gain[:, col]).astype(BF16)
     ga[z, x, y] = normed[:, 0:640]
     gb[z, x, y] = normed[:, 640:1280]
-    gc[z, x, y, :, 0:512] = normed[:, 1280:1792]
+    gc[z, x, y] = normed[:, 1280:1792]
     lane16 = lax.broadcasted_iota(jnp.int32, (16, 128), 1)
     high = e16.astype(BF16).astype(F32)
-    gc[z, x, y, :, 512:640] = jnp.where(lane16 < EXPERTS, high, e16 - high).astype(BF16)
+    gx[x, y] = jnp.where(lane16 < EXPERTS, high, e16 - high).astype(BF16)
 
     gathered = (ga, gb, gc)
 
@@ -310,42 +307,43 @@
     def gate_up_slice(zz, first=False):
         k = pl.ds(pl.multiple_of(BASE[0] + zz * WIDTH[0], 128), WIDTH[0])
 
-        @pl.loop(0, 2)
-        def _(n):
-            cols = pl.ds(pl.multiple_of(n * 512, 512), 512)
-            rows = ga[zz].reshape(256, WIDTH[0])
-            out = jnp.dot(rows, wgu[k, cols], preferred_element_type=F32).reshape(4, 4, 16, 512)
-            acc[..., cols] = out if first else acc[..., cols] + out
-
-    def gate_up_rows(*ds):
-        for p in (1, 2):
-            picks = []
-            for d in ds:
-                axis = GATHER[p][2]
-                picks.append((plus("x", d), slice(None)) if axis == "x" else (slice(None), plus("y", d)))
-
-            @pl.loop(0, 1)
-            def _(n, p=p, picks=picks):
-                cols = pl.ds(pl.multiple_of(n * 1024, 1024), 1024)
-                rows = [
-                    jnp.concatenate(
-                        [gathered[p][i, a, b, :, 0 : WIDTH[p]].reshape(64, WIDTH[p]) for i in range(4)], axis=1
-                    )
-                    for a, b in picks
-                ]
-                rows = jnp.concatenate(rows, axis=0) if len(rows) > 1 else rows[0]
-                out = jnp.dot(rows, wgu[pl.ds(BASE[p], 4 * WIDTH[p]), cols], preferred_element_type=F32)
-                for i, (a, b) in enumerate(picks):
-                    acc[a, b, :, cols] += out[64 * i : 64 * i + 64].reshape(4, 16, 1024)
+        rows = ga[zz].reshape(256, WIDTH[0])
+        out = jnp.dot(rows, wgu[k, :], preferred_element_type=F32).reshape(4, 4, 16, 2 * FFD)
+        acc[...] = out if first else acc[...] + out
+
+    def gate_up_rows(p, *ds):
+        picks = []
+        for d in ds:
+            axis = GATHER[p][2]
+            picks.append((plus("x", d), slice(None)) if axis == "x" else (slice(None), plus("y", d)))
+
+        rows = [
+            jnp.concatenate([gathered[p][i, a, b].reshape(64, WIDTH[p]) for i in range(4)], axis=1) for a, b in picks
+        ]
+        rows = jnp.concatenate(rows, axis=0) if len(rows) > 1 else rows[0]
+        out = jnp.dot(rows, wgu[pl.ds(BASE[p], 4 * WIDTH[p]), :], preferred_element_type=F32)
+        for i, (a, b) in enumerate(picks):
+            acc[a, b] += out[64 * i : 64 * i + 64].reshape(4, 16, 2 * FFD)
+
+    def table_start(k):
+        here = gx.at[x, y] if k == 0 else gx.at[:, y]
+        return [go(remote(here, here, near("xy"[k], d))) for d in (2, 1, 3)]
 
     for p in range(3):
         gather_start(p, 0)
+    table_copies = table_start(0)
     load_q.wait()
     load_c.wait()
     attend(0, 4)
     for p in range(3):
         gather_wait(p, 3)
         gather_start(p, 1)
+    for copy in table_copies:
+        copy.wait_recv()
+    table_copies = table_start(1)
+    for p, i in pieces:
+        here, there = pl.ds(i * SLICE + OFF[p], WIDTH[p]), pl.ds(BASE[p] + i * WIDTH[p], WIDTH[p])
+        load_d.append(load(w_down.at[:, here], wd.at[:, there]))
     attend(4, 8)
     store_summed = load(summed, summed_out)
     for p in range(3):
@@ -356,33 +354,38 @@
     for copy in load_gu:
         copy.wait()
     gate_up_slice(z, True)
-    gate_up_rows(0)
-    for p in range(3):
+    gate_up_rows(1, 0)
+    gate_up_rows(2, 0)
+    for p in (2, 0, 1):
         gather_forward(p, 2)
     latent_step(lambda one, two, three, share: [c.wait_recv() for c in one] + [c.start() for c in two])
-    for p in range(3):
-        gather_wait(p, 2)
+    gather_wait(2, 2)
+    gate_up_rows(2, 1, 3)
+    gather_wait(0, 2)
     gate_up_slice(plus("z", 1))
     gate_up_slice(plus("z", 3))
-    gate_up_rows(1, 3)
+    gather_wait(1, 2)
+    gate_up_rows(1, 1, 3)
+    gather_wait(2, 2)
+    gate_up_rows(2, 2)
     gather_wait(0, 2)
     gate_up_slice(plus("z", 2))
     gather_wait(1, 2)
-    gather_wait(2, 2)
-    gate_up_rows(2)
-
+    gate_up_rows(1, 2)
+
+    for copy in table_copies:
+        copy.wait_recv()
     expert = z * 4 + y
     mine = lax.broadcasted_iota(jnp.int32, (256, 128), 1)
     mine = jnp.logical_or(mine == expert, mine == expert + EXPERTS)
-    table_all = gc[0, :, :, :, 512:640].reshape(256, 128).astype(F32)
+    table_all = gx[...].reshape(256, 128).astype(F32)
     gate_col[...] = jnp.sum(jnp.where(mine, table_all, 0.0), axis=1, keepdims=True)
 
-    @pl.loop(0, 8)
+    @pl.loop(0, 4)
     def _(i):
-        rows = pl.ds(pl.multiple_of(i * 32, 32), 32)
-        half = pl.ds(pl.multiple_of(lax.rem(i, 2) * 2, 2), 2)
-        g = acc[i // 2, half, :, 0:FFD].reshape(32, FFD)
-        u = acc[i // 2, half, :, FFD:].reshape(32, FFD)
+        rows = pl.ds(pl.multiple_of(i * 64, 64), 64)
+        g = acc[i, :, :, 0:FFD].reshape(64, FFD)
+        u = acc[i, :, :, FFD:].reshape(64, FFD)
         act[rows, :] = (g / (1.0 + jnp.exp(-g)) * u * gate_col[rows, :]).astype(BF16)
 
     for copy in load_d:
@@ -581,8 +584,7 @@
 def merge(new_latent, factors, summed, latent_out, context):
     latent_out[...] = new_latent[...]
     rows = new_latent[:, 0:LAT].astype(F32)
-    rows = jnp.where(pl.program_id(0) == 0, rows[0:4], rows[4:8])
-    for i in range(4):
+    for i in range(8):
         row = rows[i : i + 1]
         context[i] = (factors[i, :, 0:1] * summed[i] + factors[i, :, 64:65] * row).astype(BF16)
 
@@ -644,9 +646,10 @@
         v((4, 4, SLICE), BF16),
         v((4, 4, 128), F32),
         v((16, SLICE), F32),
-        v((4, 4, 4, 16, 640), BF16),
-        v((4, 4, 4, 16, 640), BF16),
-        v((4, 4, 4, 16, 640), BF16),
+        v((4, 4, 4, 16, WIDTH[0]), BF16),
+        v((4, 4, 4, 16, WIDTH[1]), BF16),
+        v((4, 4, 4, 16, WIDTH[2]), BF16),
+        v((4, 4, 16, 128), BF16),
         v((4, 4, 16, 2 * FFD), F32),
         v((256, 1), F32),
         v((256, FFD), BF16),
@@ -693,19 +696,19 @@
     )
     return pl.pallas_call(
         merge,
-        grid=(2,),
+        grid=(1,),
         out_shape=(
             jax.ShapeDtypeStruct((8, KVW), BF16),
             jax.ShapeDtypeStruct((8, 64, LAT), BF16),
         ),
         in_specs=[
             pl.BlockSpec((8, KVW), lambda i: (0, 0)),
-            pl.BlockSpec((4, 64, 128), lambda i: (i, 0, 0)),
-            pl.BlockSpec((4, 64, LAT), lambda i: (i, 0, 0)),
+            pl.BlockSpec((8, 64, 128), lambda i: (i, 0, 0)),
+            pl.BlockSpec((8, 64, LAT), lambda i: (i, 0, 0)),
         ],
         out_specs=(
             pl.BlockSpec((8, KVW), lambda i: (0, 0)),
-            pl.BlockSpec((4, 64, LAT), lambda i: (i, 0, 0)),
+            pl.BlockSpec((8, 64, LAT), lambda i: (i, 0, 0)),
         ),
     )(*state)
 

time: 69.8 us -> 68.4 us (0.980)
  Pallas kernels: 69 us -> 67.6 us
    pallas_call x1, Pallas kernels: 66.8 us -> 65.3 us  [shards(): pl.pallas_call(kernel, out_shape=(jax.ShapeDtypeStruct((8, KVW), BF16), j...]
where the time goes in v4:
time: 68.4 us; the launch traced here: 68.3 us
  Pallas kernels  67.6 us (99%)
    pallas_call x1, Pallas kernels, shards(): pl.pallas_call(kernel, out_shape=(jax.ShapeDtypeStruct((8, KVW), BF16), j...  65.3 us
    pallas_call x1, Pallas kernels, shards(): pl.pallas_call(merge, grid=(1,), out_shape=(jax.ShapeDtypeStruct((8, KVW)...  2.36 us

profile of v4, /device:TPU:1, one launch (start us, length us, event | category | flops | bytes accessed | tf_op | source)
XLA Modules:
  0.0 68.3 jit_solution(16128493104251479112)
XLA Ops:
  0.6 65.3 %shard_map.140 = (bf16[8,576]{1,0:T(8,128)(2,1)}, f32[8,64,128]{2,1,0:T(8,128)}, f32[8,64,512]{2,1,0:T(8,128)}) custom-call(bf16[8,7168]{1,0:T(8,128)(2,1)} %hidden_in.1, s32[8,8]{1,0:T(8,128)} %ids_in.1, f32[8,8]{1,0:T(8,128)} %gates_in.1, f32[1,7168]{1,0:T(1,128)} %bitcast.7, f32[1,7168]{1,0:T(1,128)} %bitcast.8, f32[1,512]{1,0:T(1,128)} %bitcast.9, ...), custom_call_target="tpu_custom_call" | custom-call | flops 6000000000 | bytes 26000000 | tf_op jit(solution)/shard_map/pallas_call | solution.py:666
  65.9 2.4 %shard_map.141 = (bf16[8,576]{1,0:T(8,128)(2,1)}, bf16[8,64,512]{2,1,0:T(8,128)(2,1)}) custom-call(bf16[8,576]{1,0:T(8,128)(2,1)} %get-tuple-element.5.new_latent, f32[8,64,128]{2,1,0:T(8,128)} %get-tuple-element.6.factors, f32[8,64,512]{2,1,0:T(8,128)} %get-tuple-element.7.summed), custom_call_target="tpu_custom_call" | custom-call | tf_op jit(solution)/shard_map/pallas_call | solution.py:697

commit v5 on v4

--- a/solution.py
+++ b/solution.py
@@ -471,10 +471,11 @@
     down(0, plus("z", 1))
     down(0, plus("z", 3))
     scatter_direct(0, 0, oa)
+    cur = list(outs)
+    for p in range(3):
+        scatter_forward(p, 0, cur[p])
     down(0, z)
-    cur = list(outs)
-    for p in range(3):
-        scatter_forward(p, 0, cur[p])
+
     def scatter_all(p, s):
         order = SCATTER[p]
         b = order[s]

time: 68.4 us -> 68.4 us (level)
  no operation moved by 1% of the time
where the time goes in v5:
time: 68.4 us; the launch traced here: 68.3 us
  Pallas kernels  67.6 us (99%)
    pallas_call x1, Pallas kernels, shards(): pl.pallas_call(kernel, out_shape=(jax.ShapeDtypeStruct((8, KVW), BF16), j...  65.3 us
    pallas_call x1, Pallas kernels, shards(): pl.pallas_call(merge, grid=(1,), out_shape=(jax.ShapeDtypeStruct((8, KVW)...  2.36 us

profile of v5, /device:TPU:1, one launch (start us, length us, event | category | flops | bytes accessed | tf_op | source)
XLA Modules:
  0.0 68.3 jit_solution(2245821530530096420)
XLA Ops:
  0.6 65.3 %shard_map.140 = (bf16[8,576]{1,0:T(8,128)(2,1)}, f32[8,64,128]{2,1,0:T(8,128)}, f32[8,64,512]{2,1,0:T(8,128)}) custom-call(bf16[8,7168]{1,0:T(8,128)(2,1)} %hidden_in.1, s32[8,8]{1,0:T(8,128)} %ids_in.1, f32[8,8]{1,0:T(8,128)} %gates_in.1, f32[1,7168]{1,0:T(1,128)} %bitcast.7, f32[1,7168]{1,0:T(1,128)} %bitcast.8, f32[1,512]{1,0:T(1,128)} %bitcast.9, ...), custom_call_target="tpu_custom_call" | custom-call | flops 6000000000 | bytes 26000000 | tf_op jit(solution)/shard_map/pallas_call | solution.py:667
  65.9 2.4 %shard_map.141 = (bf16[8,576]{1,0:T(8,128)(2,1)}, bf16[8,64,512]{2,1,0:T(8,128)(2,1)}) custom-call(bf16[8,576]{1,0:T(8,128)(2,1)} %get-tuple-element.5.new_latent, f32[8,64,128]{2,1,0:T(8,128)} %get-tuple-element.6.factors, f32[8,64,512]{2,1,0:T(8,128)} %get-tuple-element.7.summed), custom_call_target="tpu_custom_call" | custom-call | tf_op jit(solution)/shard_map/pallas_call | solution.py:698
